TPU v7x, 32 devices: a whole 2x2x4 slice. The times are simulated.
32 devices in a mesh: dp: 16 (over z, x, core), seq: 2 (over y).
Axes of the slice: x: 2, y: 2, z: 4, core: 2. Of those that a mesh axis runs over, the one named last changes fastest.
Arguments:
- tokens: bfloat16 [32, 1024, 768], P('dp', 'seq'), may hold values from -6 to 6
- time_embedding: bfloat16 [32, 128], P('dp'), may hold values from -6 to 6
- prefix_length: int32 [32], P('dp'), may hold values from 0 to 511
- suffix_mask: int32 [32, 1024], P('dp', 'seq'), may hold values 0 or 1
- cotangent: bfloat16 [32, 1024, 768], P('dp', 'seq'), may hold values from -6 to 6
- modulation_weight: bfloat16 [4608, 128], replicated, may hold values from -0.5 to 0.5
- modulation_bias: bfloat16 [4608], replicated, may hold values from -3 to 3
- attention_gain: bfloat16 [768], replicated, may hold values from 0.099609375 to 1.8984375
- attention_in: bfloat16 [768, 2304], replicated, may hold values from -0.15625 to 0.15625
- attention_out: bfloat16 [768, 768], replicated, may hold values from -1.75 to 1.75
- feed_gain: bfloat16 [768], replicated, may hold values from 0.099609375 to 1.8984375
- feed_up: bfloat16 [768, 3072], replicated, may hold values from -0.21875 to 0.21875
- feed_up_bias: bfloat16 [3072], replicated, may hold values from -3 to 3
- feed_down: bfloat16 [3072, 768], replicated, may hold values from -0.109375 to 0.109375
- feed_down_bias: bfloat16 [768], replicated, may hold values from -3 to 3
Outputs:
- block_output: bfloat16 [32, 1024, 768], P('dp', 'seq')
- tokens_grad: bfloat16 [32, 1024, 768], P('dp', 'seq')
- time_grad: float32 [32, 128], P('dp')
- modulation_weight_grad: float32 [4608, 128], P('dp')
- modulation_bias_grad: float32 [4608], P('dp')
- attention_gain_grad: float32 [768], P('dp')
- attention_in_grad: float32 [768, 2304], P('dp')
- attention_out_grad: float32 [768, 768], P('dp')
- feed_gain_grad: float32 [768], P('dp')
- feed_up_grad: float32 [768, 3072], P('dp')
- feed_up_bias_grad: float32 [3072], P('dp')
- feed_down_grad: float32 [3072, 768], P('dp')
- feed_down_bias_grad: float32 [768], P('dp')
All inputs are finite; a program needn't handle non-finite values. No bound on the sum of `suffix_mask` on one device may be relied on, other than what follows from the above.
Results may differ from a plain program's by a relative error of at most 0.015.
The roundings to bfloat16 on the way count: a program that leaves them out, or rounds other values in their place, can miss the bound.
Values may be sent and summed in bfloat16 or wider, within the bound.
A program may use at most 256 MiB of HBM per device.

v0:
```python
import functools
from functools import partial

import jax
import jax.numpy as jnp
import numpy as np
from jax import lax
from jax.experimental import pallas as pl
from jax.experimental.pallas import tpu as pltpu
from jax.sharding import PartitionSpec as P

HEADS = 12
HD = 64


highest = lax.Precision.HIGHEST


def as_sent(shard):

    def short(part):
        return part.astype(jnp.bfloat16) if part.dtype == jnp.float32 else part

    return jax.tree.map(short, shard)


def normalize(values):
    centre = values - jnp.mean(values, -1, keepdims=True)
    spread = jnp.mean(centre * centre, -1, keepdims=True)
    return centre * lax.rsqrt(spread + 1e-05)


def modulate(values, scaling, shifts, scales):
    return normalize(values) * scaling * (1.0 + scales) + shifts


def rotate(values, cosine, sines, direction):
    halves = values.shape[-1] // 2
    former = values[..., :halves]
    latter = values[..., halves:]
    cosine = cosine[None, :, None, :]
    sines = direction * sines[None, :, None, :]
    return jnp.concatenate([former * cosine - latter * sines, latter * cosine + former * sines], -1)


def attend_forward(stacked):
    query_rows = stacked[:, 0]
    key_rows = stacked[:, 1]
    value_rows = stacked[:, 2]
    length = query_rows.shape[0]
    block_rows = min(512, length)
    pieces = []
    logsums = []
    for offset in range(0, length, block_rows):
        query_block = query_rows[offset : offset + block_rows]
        scores = (
            jnp.einsum("qhd,khd->hqk", query_block, key_rows, preferred_element_type=jnp.float32)
            * 0.125
        )
        largest = jnp.max(scores, -1, keepdims=True)
        exponentials = jnp.exp(scores - largest)
        totals = jnp.sum(exponentials, -1, keepdims=True)
        probability = (exponentials / totals).astype(jnp.bfloat16)
        pieces.append(
            jnp.einsum("hqk,khd->qhd", probability, value_rows, preferred_element_type=jnp.float32)
        )
        logsums.append((largest + jnp.log(totals))[..., 0])
    return (jnp.concatenate(pieces, 0).astype(jnp.bfloat16), jnp.concatenate(logsums, 1))


def attend_backward(operands):
    stacked, grad_attended, logsums = operands
    query_rows = stacked[:, 0]
    key_rows = stacked[:, 1]
    value_rows = stacked[:, 2]
    length = query_rows.shape[0]
    block_rows = min(512, length)
    grad_query = []
    grad_keys = jnp.zeros(key_rows.shape, jnp.float32)
    grad_values = jnp.zeros(value_rows.shape, jnp.float32)
    for offset in range(0, length, block_rows):
        query_block = query_rows[offset : offset + block_rows]
        grad_block = grad_attended[offset : offset + block_rows]
        scores = (
            jnp.einsum("qhd,khd->hqk", query_block, key_rows, preferred_element_type=jnp.float32)
            * 0.125
        )
        probability = jnp.exp(scores - logsums[:, offset : offset + block_rows, None])
        grad_probs = jnp.einsum(
            "qhd,khd->hqk", grad_block, value_rows, preferred_element_type=jnp.float32
        )
        row_dots = jnp.sum(probability * grad_probs, -1, keepdims=True)
        grad_scores = (probability * (grad_probs - row_dots)).astype(jnp.bfloat16)
        grad_query.append(
            (
                jnp.einsum(
                    "hqk,khd->qhd", grad_scores, key_rows, preferred_element_type=jnp.float32
                )
                * 0.125
            ).astype(jnp.bfloat16)
        )
        grad_keys = grad_keys + jnp.einsum(
            "hqk,qhd->khd", grad_scores, query_block, preferred_element_type=jnp.float32
        )
        grad_values = grad_values + jnp.einsum(
            "hqk,qhd->khd",
            probability.astype(jnp.bfloat16),
            grad_block,
            preferred_element_type=jnp.float32,
        )
    return jnp.stack(
        [
            jnp.concatenate(grad_query, 0),
            (grad_keys * 0.125).astype(jnp.bfloat16),
            grad_values.astype(jnp.bfloat16),
        ],
        1,
    )


def general_body(
    tokens,
    time_embedding,
    prefix_length,
    suffix_mask,
    cotangent,
    modulation_weight,
    modulation_bias,
    attention_gain,
    attention_in,
    attention_out,
    feed_gain,
    feed_up,
    feed_up_bias,
    feed_down,
    feed_down_bias,
):
    sequences, local_len, model_width = tokens.shape
    groups = lax.axis_size("seq")
    data_size = lax.axis_size("dp")
    length = local_len * groups
    heads_local = HEADS // groups
    group_width = model_width // groups
    modulation = jnp.einsum(
        "sc,oc->so", time_embedding, modulation_weight, preferred_element_type=jnp.float32
    ) + modulation_bias.astype(jnp.float32)
    shift_one, scale_one, gate_one, shift_two, scale_two, gate_two = [
        portion[:, None, :] for portion in jnp.split(modulation, 6, axis=1)
    ]
    inputs = tokens.astype(jnp.float32)
    first_float, first_back = jax.vjp(
        modulate, inputs, attention_gain.astype(jnp.float32), shift_one, scale_one
    )
    first_input = first_float.astype(jnp.bfloat16)
    projected = jnp.einsum(
        "spd,de->spe", first_input, attention_in, preferred_element_type=jnp.float32
    ).reshape(sequences, local_len, 3, HEADS, HD)
    position_ints = lax.axis_index("seq") * local_len + jnp.arange(local_len, dtype=jnp.int32)
    positions = position_ints.astype(jnp.float32)
    inverse = 10000.0 ** (-jnp.arange(HD // 2, dtype=jnp.float32) * 2.0 / HD)
    angles = positions[:, None] * inverse[None, :]
    cosine = jnp.cos(angles)
    sines = jnp.sin(angles)
    rotated = jnp.stack(
        [
            rotate(projected[:, :, 0], cosine, sines, 1.0),
            rotate(projected[:, :, 1], cosine, sines, 1.0),
            projected[:, :, 2],
        ],
        2,
    ).astype(jnp.bfloat16)
    by_heads = lax.all_to_all(
        rotated.reshape(sequences, local_len, 3, groups, group_width),
        "seq",
        split_axis=3,
        concat_axis=1,
        tiled=True,
    )
    by_heads = by_heads.reshape(sequences, length, 3, heads_local, HD)
    attended_heads, logsums = lax.map(attend_forward, by_heads)
    attended = lax.all_to_all(
        as_sent(attended_heads.reshape(sequences, length, 1, group_width)),
        "seq",
        split_axis=1,
        concat_axis=2,
        tiled=True,
    )
    attended = attended.reshape(sequences, local_len, model_width)
    branch_one = jnp.einsum(
        "spd,de->spe", attended, attention_out, preferred_element_type=jnp.float32
    )
    middle = inputs + gate_one * branch_one
    second_float, second_back = jax.vjp(
        modulate, middle, feed_gain.astype(jnp.float32), shift_two, scale_two
    )
    second_input = second_float.astype(jnp.bfloat16)
    hidden = jnp.einsum(
        "spd,df->spf", second_input, feed_up, preferred_element_type=jnp.float32
    ) + feed_up_bias.astype(jnp.float32)
    activated_float, gelu_back = jax.vjp(partial(jax.nn.gelu, approximate=True), hidden)
    activated = activated_float.astype(jnp.bfloat16)
    branch_two = jnp.einsum(
        "spf,fd->spd", activated, feed_down, preferred_element_type=jnp.float32
    ) + feed_down_bias.astype(jnp.float32)
    block_output = (middle + gate_two * branch_two).astype(jnp.bfloat16)
    live_rows = ((position_ints[None, :] >= prefix_length[:, None]) & (suffix_mask == 1)).astype(
        jnp.float32
    )
    grad_output = cotangent.astype(jnp.float32) * live_rows[:, :, None]
    grad_gate_two = jnp.sum(grad_output * branch_two, axis=1)
    grad_branch_two = (gate_two * grad_output).astype(jnp.bfloat16)
    feed_down_bias_grad = jnp.sum(grad_branch_two.astype(jnp.float32), axis=(0, 1))
    feed_down_grad = jnp.einsum(
        "spf,spd->fd", activated, grad_branch_two, preferred_element_type=jnp.float32
    )
    grad_activated = jnp.einsum(
        "spd,fd->spf", grad_branch_two, feed_down, preferred_element_type=jnp.float32
    )
    grad_hidden = gelu_back(grad_activated)[0].astype(jnp.bfloat16)
    feed_up_bias_grad = jnp.sum(grad_hidden.astype(jnp.float32), axis=(0, 1))
    feed_up_grad = jnp.einsum(
        "spd,spf->df", second_input, grad_hidden, preferred_element_type=jnp.float32
    )
    grad_second = jnp.einsum(
        "spf,df->spd", grad_hidden, feed_up, preferred_element_type=jnp.float32
    )
    grad_from_norm, feed_gain_grad, grad_shift_two, grad_scale_two = second_back(grad_second)
    grad_middle = grad_output + grad_from_norm
    grad_gate_one = jnp.sum(grad_middle * branch_one, axis=1)
    grad_branch_one = (gate_one * grad_middle).astype(jnp.bfloat16)
    attention_out_grad = jnp.einsum(
        "spd,spe->de", attended, grad_branch_one, preferred_element_type=jnp.float32
    )
    grad_attended = jnp.einsum(
        "spe,de->spd", grad_branch_one, attention_out, preferred_element_type=jnp.float32
    ).astype(jnp.bfloat16)
    grad_heads = lax.all_to_all(
        grad_attended.reshape(sequences, local_len, groups, group_width),
        "seq",
        split_axis=2,
        concat_axis=1,
        tiled=True,
    )
    grad_heads = grad_heads.reshape(sequences, length, heads_local, HD)
    grad_stacked = lax.map(attend_backward, (by_heads, grad_heads, logsums))
    grad_positions = lax.all_to_all(
        as_sent(grad_stacked.reshape(sequences, length, 3, 1, group_width)),
        "seq",
        split_axis=1,
        concat_axis=3,
        tiled=True,
    )
    grad_positions = grad_positions.reshape(sequences, local_len, 3, HEADS, HD).astype(jnp.float32)
    grad_projected = jnp.stack(
        [
            rotate(grad_positions[:, :, 0], cosine, sines, -1.0),
            rotate(grad_positions[:, :, 1], cosine, sines, -1.0),
            grad_positions[:, :, 2],
        ],
        2,
    ).astype(jnp.bfloat16)
    grad_projected = grad_projected.reshape(sequences, local_len, 3 * model_width)
    attention_in_grad = jnp.einsum(
        "spd,spe->de", first_input, grad_projected, preferred_element_type=jnp.float32
    )
    grad_first = jnp.einsum(
        "spe,de->spd", grad_projected, attention_in, preferred_element_type=jnp.float32
    )
    grad_tokens_norm, attention_gain_grad, grad_shift_one, grad_scale_one = first_back(grad_first)
    tokens_grad = (grad_middle + grad_tokens_norm).astype(jnp.bfloat16)
    grad_modulation = jnp.concatenate(
        [
            grad_shift_one[:, 0],
            grad_scale_one[:, 0],
            grad_gate_one,
            grad_shift_two[:, 0],
            grad_scale_two[:, 0],
            grad_gate_two,
        ],
        1,
    )
    modulation_total = lax.psum(grad_modulation.astype(jnp.bfloat16), "seq").astype(jnp.float32)
    time_grad = jnp.einsum(
        "so,oc->sc", modulation_total, modulation_weight.astype(jnp.float32), precision=highest
    )
    modulation_weight_grad = jnp.einsum(
        "so,sc->oc", grad_modulation, time_embedding.astype(jnp.float32), precision=highest
    )
    modulation_bias_grad = jnp.sum(grad_modulation, axis=0)
    gradients = (
        modulation_weight_grad,
        modulation_bias_grad,
        attention_gain_grad,
        attention_in_grad,
        attention_out_grad,
        feed_gain_grad,
        feed_up_grad,
        feed_up_bias_grad,
        feed_down_grad,
        feed_down_bias_grad,
    )
    flattened = tuple((g.reshape(data_size, -1) for g in gradients))
    shares = lax.psum_scatter(flattened, "dp", scatter_dimension=0, tiled=True)
    summed = jax.tree.map(lambda part: part.astype(jnp.float32), lax.psum(as_sent(shares), "seq"))
    shards = tuple(
        (s.reshape((g.shape[0] // data_size,) + g.shape[1:]) for s, g in zip(summed, gradients))
    )
    return (
        block_output,
        tokens_grad,
        time_grad,
        shards[0],
        shards[1],
        shards[2],
        shards[3],
        shards[4],
        shards[5],
        shards[6],
        shards[7],
        shards[8],
        shards[9],
    )


T_ROWS = 256
MIB = 1 << 20


def dot(a, b, ca, cb):
    return lax.dot_general(a, b, (((ca,), (cb,)), ((), ())), preferred_element_type=jnp.float32)


def params(limit=60):
    return pltpu.CompilerParams(vmem_limit_bytes=limit * MIB)


def norm_rows(values):
    centre = values - jnp.mean(values, -1, keepdims=True)
    inverse = lax.rsqrt(jnp.mean(centre * centre, -1, keepdims=True) + 1e-05)
    return centre * inverse, inverse


def swap_halves(values, lane):
    left = pltpu.roll(values, 96, 1)
    right = pltpu.roll(values, 32, 1)
    return jnp.where(lane % 64 < 32, left, right)


def project_kernel(source_ref, mod_ref, gain_ref, weight_ref, cos_ref, sin_ref, first_t_ref, qkv_ref):
    rows, model = source_ref.shape
    lane = lax.broadcasted_iota(jnp.int32, (rows, 128), 1)
    scaling = gain_ref[...] * (1.0 + mod_ref[1:2])
    normed, _ = norm_rows(source_ref[...].astype(jnp.float32))
    first = (normed * scaling + mod_ref[0:1]).astype(jnp.bfloat16)
    first_t_ref[...] = first.T
    for part in range(3):
        projected = dot(first, weight_ref[:, part * model : (part + 1) * model], 1, 0)
        for block in range(model // 128):
            piece = projected[:, block * 128 : (block + 1) * 128]
            if part < 2:
                piece = piece * cos_ref[...] + swap_halves(piece, lane) * sin_ref[...]
            piece = piece.astype(jnp.bfloat16)
            if part == 0:
                piece = piece * 0.125
            column = part * model + block * 128
            qkv_ref[:, column : column + 128] = piece


def attend_kernel(q_ref, k_ref, v_ref, out_ref, exp_ref, inv_ref):
    rows = T_ROWS
    length = q_ref.shape[0]
    lane = lax.broadcasted_iota(jnp.int32, (rows, 128), 1)
    keys = k_ref[...]
    values = jnp.concatenate([v_ref[...], jnp.ones((length, 128), jnp.bfloat16)], 1)
    for chunk in range(length // rows):
        at = slice(chunk * rows, (chunk + 1) * rows)
        queries = q_ref[at]
        outs = []
        inverses = []
        for head in range(2):
            mine = jnp.where((lane < 64) == (head == 0), queries, jnp.zeros_like(queries))
            scores = dot(mine, keys, 1, 1)
            largest = jnp.max(scores, -1, keepdims=True)
            exps = jnp.exp(scores - largest).astype(jnp.bfloat16)
            exp_ref[head, at] = exps
            summed = dot(exps, values, 1, 0)
            inverse = 1.0 / summed[:, 128:256]
            outs.append(summed[:, 0:128] * inverse)
            inverses.append(inverse)
        out_ref[at] = jnp.where(lane < 64, outs[0], outs[1]).astype(jnp.bfloat16)
        inv_ref[at] = jnp.where(lane < 64, inverses[0], inverses[1])


def share(core, grad, keep_ref, send_ref, *at):
    first, second = grad
    keep_ref[at] = jnp.where(core == 0, first, second)
    send_ref[at] = jnp.where(core == 0, second, first)


def middle_kernel(
    core_ref,
    own_ref,
    other_ref,
    own_cot_ref,
    other_cot_ref,
    attended_ref,
    mod_ref,
    gain_ref,
    out_weight_ref,
    up_ref,
    up_bias_ref,
    down_ref,
    down_bias_ref,
    own_out_ref,
    other_out_ref,
    grad_middle_ref,
    grad_attended_ref,
    rows_ref,
    up_bias_grad_ref,
    down_keep_ref,
    down_send_ref,
    up_keep_ref,
    up_send_ref,
    out_keep_ref,
    out_send_ref,
    branch_one,
    attended_t,
    second,
    second_t,
    grad_two,
    sum_two,
    sum_second,
    act_t,
    grad_hidden,
):
    rows = T_ROWS
    step = pl.program_id(0)
    core = core_ref[0]
    half, model = own_ref.shape
    length = 2 * half
    scaling = gain_ref[...] * (1.0 + mod_ref[4:5])
    gate_one = mod_ref[2:3]
    shift_two = mod_ref[3:4]
    gate_two = mod_ref[5:6]

    def pick(first_ref, second_ref, chunk):
        at = chunk * rows
        return (first_ref if at < half else second_ref)[at % half : at % half + rows]

    @pl.when(step == 0)
    def _():
        bias_grad = jnp.zeros((1, model), jnp.float32)
        for chunk in range(length // rows):
            at = slice(chunk * rows, (chunk + 1) * rows)
            branch = dot(attended_ref[at], out_weight_ref[...], 1, 0)
            branch_one[at] = branch
            attended_t[:, at] = attended_ref[at].T
            sum_two[at] = jnp.zeros((rows, model), jnp.float32)
            sum_second[at] = jnp.zeros((rows, model), jnp.float32)
            middle = pick(own_ref, other_ref, chunk).astype(jnp.float32) + gate_one * branch
            normed, _ = norm_rows(middle)
            rounded = (normed * scaling + shift_two).astype(jnp.bfloat16)
            second[at] = rounded
            second_t[:, at] = rounded.T
            grad = (gate_two * pick(own_cot_ref, other_cot_ref, chunk).astype(jnp.float32)).astype(jnp.bfloat16)
            grad_two[at] = grad
            bias_grad = bias_grad + jnp.sum(grad.astype(jnp.float32), 0, keepdims=True)
        rows_ref[5:6] = bias_grad

    up = up_ref[...]
    down = down_ref[...]
    width = up.shape[1]
    bias_sum = jnp.zeros((1, width), jnp.float32)
    for chunk in range(length // rows):
        at = slice(chunk * rows, (chunk + 1) * rows)
        hidden = dot(second[at], up, 1, 0) + up_bias_ref[...]
        squared = hidden * hidden
        tanh = jnp.tanh(hidden * (0.7978845608028654 + 0.035677408136300125 * squared))
        gate = 0.5 + 0.5 * tanh
        activated = (hidden * gate).astype(jnp.bfloat16)
        slope = gate + (0.5 * hidden) * (1.0 - tanh * tanh) * (0.7978845608028654 + 0.10703222440890037 * squared)
        act_t[:, at] = activated.T
        grad = (slope * dot(grad_two[at], down, 1, 1)).astype(jnp.bfloat16)
        grad_hidden[at] = grad
        bias_sum = bias_sum + jnp.sum(grad.astype(jnp.float32), 0, keepdims=True)
        sum_two[at] += dot(activated, down, 1, 0)
        sum_second[at] += dot(grad, up, 1, 1)

    up_bias_grad_ref[...] = bias_sum
    down_grad = dot(act_t[...], grad_two[...], 1, 0).astype(jnp.bfloat16).reshape(down_keep_ref.shape[0], 2, -1, model)
    share(core, (down_grad[:, 0], down_grad[:, 1]), down_keep_ref, down_send_ref, Ellipsis)
    up_grad = dot(second_t[...], grad_hidden[...], 1, 0).astype(jnp.bfloat16).reshape(up_keep_ref.shape[0], 2, -1, width)
    share(core, (up_grad[:, 0], up_grad[:, 1]), up_keep_ref, up_send_ref, Ellipsis)

    @pl.when(step == pl.num_programs(0) - 1)
    def _():
        sums = [jnp.zeros((1, model), jnp.float32) for _ in range(4)]
        for chunk in range(length // rows):
            at = slice(chunk * rows, (chunk + 1) * rows)
            branch = branch_one[at]
            middle = pick(own_ref, other_ref, chunk).astype(jnp.float32) + gate_one * branch
            normed, inverse = norm_rows(middle)
            branch_two = sum_two[at] + down_bias_ref[...]
            output = (middle + gate_two * branch_two).astype(jnp.bfloat16)
            place = (chunk * rows) % half
            (own_out_ref if chunk * rows < half else other_out_ref)[place : place + rows] = output
            cot = pick(own_cot_ref, other_cot_ref, chunk).astype(jnp.float32)
            grad = sum_second[at]
            weighted = grad * normed
            scaled = grad * scaling
            inner = jnp.mean(weighted * scaling, -1, keepdims=True)
            grad_middle = cot + (scaled - jnp.mean(scaled, -1, keepdims=True) - normed * inner) * inverse
            grad_middle_ref[at] = grad_middle
            grad_one = (gate_one * grad_middle).astype(jnp.bfloat16)
            grad_two[at] = grad_one
            grad_attended_ref[at] = dot(grad_one, out_weight_ref[...], 1, 1).astype(jnp.bfloat16)
            for i, term in enumerate((grad_middle * branch, grad, weighted, cot * branch_two)):
                sums[i] = sums[i] + jnp.sum(term, 0, keepdims=True)
        rows_ref[0:1] = sums[0]
        rows_ref[1:2] = sums[1]
        rows_ref[2:3] = sums[2] * gain_ref[...]
        rows_ref[3:4] = sums[3]
        rows_ref[4:5] = sums[2] * (1.0 + mod_ref[4:5])
        out_grad = dot(attended_t[...], grad_two[...], 1, 0).astype(jnp.bfloat16)
        out_grad = out_grad.reshape(out_keep_ref.shape[0], 2, -1, model)
        share(core, (out_grad[:, 0], out_grad[:, 1]), out_keep_ref, out_send_ref, Ellipsis)


class Links:
    def __init__(self):
        dp = lax.axis_index("dp")
        self.me = lax.axis_index("seq")
        self.bit = {"C": dp % 2, "X": (dp // 2) % 2, "Z": (dp // 4) % 2, "W": (dp // 8) % 2, "Y": self.me}
        self.partner = {
            name: (dp + jump * (1 - 2 * self.bit[name]), self.me)
            for name, jump in (("C", 1), ("X", 2), ("Z", 4), ("W", 8))
        }
        self.partner["Y"] = (dp, 1 - self.me)


def remote(source, target, sems, slot, device):
    return pltpu.make_async_remote_copy(
        src_ref=source,
        dst_ref=target,
        send_sem=sems.at[0, slot],
        recv_sem=sems.at[1, slot],
        device_id=device,
        device_id_type=pl.DeviceIdType.MESH,
    )


def stage_shapes(rows, order):
    count = 8
    shapes = []
    for kind in order:
        if kind == "Y":
            rows //= 2
        else:
            count //= 2
        shapes.append((count, rows))
    shapes.append((1, rows))
    return shapes


def piece_scratch(rows, order, width, sent):
    shapes = [(8, rows)] * (3 if sent else 2)
    for shape in stage_shapes(rows, order):
        shapes += [shape] * 2
    return [pltpu.VMEM((count, r, width), jnp.bfloat16) for count, r in shapes]


class Piece:
    def __init__(self, links, refs, rows, order, sems, slot, source=None):
        refs = list(refs)
        self.links = links
        self.sems = sems
        self.slot = slot
        self.order = list(order)
        self.rows = rows
        self.split = False
        self.keep = refs.pop(0)
        first = refs.pop(0)
        self.source = source if source is not None else refs.pop(0)
        self.buffers = refs
        self.left = ["W", "Z", "X"]
        self.terms = [(self.keep, list(self.left), False)]
        copy = (self.source, first, sems, slot, links.partner["C"])
        self.slot += 1
        self.copies = [copy]
        self.flying = (copy, first, list(self.left), False)

    def launch(self, source, target, kind, bits):
        copy = (source, target, self.sems, self.slot, self.links.partner[kind])
        self.slot += 1
        remote(*copy).start()
        self.copies.append(copy)
        self.flying = (copy, target, list(bits), self.split)

    def begin(self):
        remote(*self.copies[0]).start()

    def arrive(self):
        copy, target, bits, split = self.flying
        remote(*copy).wait_recv()
        self.terms.append((target, bits, split))

    def index(self, bits, values):
        at = 0
        for bit in bits:
            at = at * 2 + values[bit]
        return at

    def add(self, out, kind):
        links = self.links
        left = [bit for bit in self.left if bit != kind]
        rows = out.shape[1]
        block = 48
        for combo in range(1 << len(left)):
            values = dict(links.bit)
            for place, bit in enumerate(left):
                values[bit] = (combo >> (len(left) - 1 - place)) & 1
            if kind is not None and kind != "Y":
                values[kind] = 1 - links.bit[kind]
            indices = [self.index(bits, values) for _, bits, _ in self.terms]

            def some(i, carry, indices=indices, combo=combo):
                start = pl.multiple_of(i * block, 16)
                total = None
                for (ref, _, split), at in zip(self.terms, indices):
                    begin = start
                    if not split and (kind == "Y" or self.split):
                        half = (1 - links.me) if kind == "Y" else links.me
                        begin = pl.multiple_of(half * rows + i * block, 16)
                    term = ref[at, pl.ds(begin, block), :].astype(jnp.float32)
                    total = term if total is None else total + term
                out[combo, pl.ds(start, block), :] = total.astype(jnp.bfloat16)
                return carry

            lax.fori_loop(0, rows // block, some, 0)

    def step(self):
        self.arrive()
        kind = self.order.pop(0)
        out, target = self.buffers.pop(0), self.buffers.pop(0)
        self.add(out, kind)
        if kind == "Y":
            self.split = True
        else:
            self.left.remove(kind)
        self.launch(out, target, kind, self.left)

    def last(self):
        self.arrive()
        self.total, self.got = self.buffers.pop(0), self.buffers.pop(0)
        self.add(self.total, None)
        self.launch(self.total, self.got, "Y", [])

    def result(self, store):
        remote(*self.flying[0]).wait_recv()
        rows = self.total.shape[1]
        total = self.total[0].astype(jnp.float32)
        got = self.got[0].astype(jnp.float32)
        if self.split:
            store(pl.ds(pl.multiple_of(self.links.me * rows, 8), rows), total)
            store(pl.ds(pl.multiple_of((1 - self.links.me) * rows, 8), rows), got)
        else:
            store(slice(0, rows), total + got)


BACK_PIECES = (("down", 192, "YXZW"), ("up", 192, "XZW"), ("out", 48, "ZXW"), ("in0", 48, "ZXW"), ("in1", 48, "ZXW"), ("in2", 48, "XZW"))
BACK_COPIES = sum(2 + len(order) for _, _, order in BACK_PIECES)


def back_kernel(
    q_ref,
    k_ref,
    v_ref,
    out_ref,
    grad_ref,
    exp_ref,
    inv_ref,
    cos_ref,
    sin_ref,
    first_t_ref,
    weight_ref,
    own_ref,
    other_ref,
    grad_middle_ref,
    mod_ref,
    gain_ref,
    down_keep,
    down_send,
    up_keep,
    up_send,
    out_keep,
    out_send,
    tokens_grad_ref,
    rows_ref,
    down_ref,
    up_ref,
    out_grad_ref,
    in_ref,
    ds_ref,
    dq_sum,
    proj,
    tokens_stage,
    sems,
    local_sems,
    *buffers,
):
    rows = T_ROWS
    step = pl.program_id(0)
    length = q_ref.shape[0]
    half, model = other_ref.shape
    links = Links()
    core = links.bit["C"]
    pieces = []
    buffers = list(buffers)
    slot = 0
    sources = [down_send, up_send, out_send, None, None, None]
    for (_, piece_rows, order), source in zip(BACK_PIECES, sources):
        count = 2 * len(order) + 4 + (source is None)
        pieces.append(Piece(links, buffers[:count], piece_rows, order, sems, slot, source))
        buffers = buffers[count:]
        slot += 2 + len(order)
    down, up, out, *ins = pieces

    def fetches():
        pairs = ((down_keep, down), (up_keep, up), (out_keep, out))
        return [pltpu.make_async_copy(s, p.keep, local_sems.at[i]) for i, (s, p) in enumerate(pairs)]

    @pl.when(step == 0)
    def _():
        barrier = pltpu.get_barrier_semaphore()
        for name in "CXZWY":
            pl.semaphore_signal(
                barrier, inc=1, device_id=links.partner[name], device_id_type=pl.DeviceIdType.MESH
            )
        pl.semaphore_wait(barrier, 5)
        for piece in (down, up, out):
            piece.begin()
        for copy in fetches():
            copy.start()

    def at_step(number):
        return pl.when(step == number)

    @at_step(2)
    def _():
        for copy in fetches():
            copy.wait()
        down.step()
        up.step()
        out.step()

    @at_step(3)
    def _():
        ins[0].step()

    @at_step(5)
    def _():
        ins[1].step()

    lane = lax.broadcasted_iota(jnp.int32, (rows, 128), 1)

    @pl.when(step < 6)
    def _():
        keys = k_ref[...]
        values = v_ref[...]
        scaled = grad_ref[...].astype(jnp.float32) * inv_ref[...]
        products = scaled * out_ref[...].astype(jnp.float32)
        scaled = scaled.astype(jnp.bfloat16)
        scaled_t = scaled.T
        queries_t = q_ref[...].T
        grad_k = []
        grad_v = []
        for head in range(2):
            for chunk in range(length // rows):
                at = slice(chunk * rows, (chunk + 1) * rows)
                mask = (lane < 64) == (head == 0)
                mine = jnp.where(mask, scaled[at], jnp.zeros((rows, 128), jnp.bfloat16))
                row_dots = jnp.sum(jnp.where(mask, products[at], 0.0), -1, keepdims=True)
                grad_p = dot(mine, values, 1, 1)
                grad_s = (exp_ref[head, at].astype(jnp.float32) * (grad_p - row_dots)).astype(jnp.bfloat16)
                ds_ref[at] = grad_s
                grad_q = dot(grad_s, keys, 1, 0) * 0.125
                if head == 0:
                    dq_sum[at] = grad_q
                else:
                    dq_sum[at] = jnp.where(lane < 64, dq_sum[at], grad_q)
            grad_v.append(dot(scaled_t[64 * head : 64 * head + 64], exp_ref[head], 1, 0))
            grad_k.append(dot(queries_t[64 * head : 64 * head + 64], ds_ref[...], 1, 0))
        columns = [pl.ds(pl.multiple_of(part * model + step * 128, 128), 128) for part in range(3)]
        proj[:, columns[2]] = jnp.concatenate(grad_v, 0).astype(jnp.bfloat16).T
        grad_keys = jnp.concatenate(grad_k, 0).astype(jnp.bfloat16).T
        for chunk in range(length // rows):
            at = slice(chunk * rows, (chunk + 1) * rows)
            for part, source in enumerate((dq_sum[at].astype(jnp.bfloat16), grad_keys[at])):
                piece = source.astype(jnp.float32)
                turned = piece * cos_ref[at] - swap_halves(piece, lane) * sin_ref[at]
                proj[at, columns[part]] = turned.astype(jnp.bfloat16)

    def weight_part(group):
        piece = ins[group]
        span = model // 3
        for part in range(3):
            column = part * model + group * span
            grad = dot(first_t_ref[...], proj[:, column : column + span], 1, 0).astype(jnp.bfloat16)
            grad = grad.reshape(8, 2, -1, span)
            share(core, (grad[:, 0], grad[:, 1]), piece.keep, piece.source, Ellipsis, slice(part * span, (part + 1) * span))
        piece.begin()

    for group in range(3):
        at_step(2 * group + 1)(functools.partial(weight_part, group))

    scaling = gain_ref[...] * (1.0 + mod_ref[1:2])

    def entry(values_ref, base):
        sums = [jnp.zeros((1, model), jnp.float32) for _ in range(2)]
        for chunk in range(half // rows):
            at = slice(base + chunk * rows, base + (chunk + 1) * rows)
            local = slice(chunk * rows, (chunk + 1) * rows)
            grad = dot(proj[at], weight_ref[...], 1, 1)
            normed, inverse = norm_rows(values_ref[local].astype(jnp.float32))
            weighted = grad * normed
            scaled = grad * scaling
            inner = jnp.mean(weighted * scaling, -1, keepdims=True)
            result = grad_middle_ref[local] + (scaled - jnp.mean(scaled, -1, keepdims=True) - normed * inner) * inverse
            tokens_stage[at] = result.astype(jnp.bfloat16)
            for i, term in enumerate((grad, weighted)):
                sums[i] = sums[i] + jnp.sum(term, 0, keepdims=True)
        return jnp.concatenate(sums, 0)

    def away():
        target = tokens_grad_ref.at[links.me]
        return remote(tokens_stage.at[pl.ds(half, half)], target, sems, BACK_COPIES, links.partner["Y"])

    def home():
        return pltpu.make_async_copy(tokens_stage.at[pl.ds(0, half)], tokens_grad_ref.at[links.me], local_sems.at[3])

    @at_step(6)
    def _():
        rows_ref[...] = entry(other_ref, half)
        away().start()
        ins[2].step()
        ins[0].step()
        ins[1].step()
        out.step()

    @at_step(7)
    def _():
        rows_ref[...] += entry(own_ref, 0)
        home().start()
        down.step()
        up.step()
        for piece in (ins[0], out, ins[1], ins[2]):
            piece.step()
        down.step()
        for piece in (ins[0], out, ins[1]):
            piece.last()
        up.step()
        ins[2].step()
        down.step()
        ins[2].last()
        down.last()
        up.last()
        span = model // 3
        for group in range(3):
            def store(at, value, group=group):
                for part in range(3):
                    column = part * model + group * span
                    in_ref[at, column : column + span] = value[:, part * span : (part + 1) * span]

            ins[group].result(store)

        def store_out(at, value):
            out_grad_ref[at] = value

        out.result(store_out)

        def store_down(at, value):
            down_ref[at] = value

        down.result(store_down)

        def store_up(at, value):
            count = up_ref.shape[0]
            for tile in range(up_ref.shape[1] // model):
                up_ref[:, tile * model : (tile + 1) * model] = value[tile * count : (tile + 1) * count]

        up.result(store_up)
        home().wait()
        away().wait()
        for piece in pieces:
            for copy in piece.copies:
                remote(*copy).wait_send()


def turn_tables(length):
    inverse = 10000.0 ** (-np.arange(HD // 2, dtype=np.float64) * 2.0 / HD)
    angles = np.arange(length, dtype=np.float64)[:, None] * inverse[None, :]
    cosine = np.tile(np.cos(angles), (1, 4))
    sines = np.sin(angles)
    sines = np.concatenate([-sines, sines, -sines, sines], 1)
    both = [np.stack([t, np.roll(t, -(length // 2), 0)]).astype(np.float32) for t in (cosine, sines)]
    return jnp.asarray(both[0]), jnp.asarray(both[1])


def call(kernel, grid, place, in_specs, out_specs, out_shape, scratch, operands, name, flops, moved, after=(), alias=()):
    count = len(in_specs) + 1
    extra = len(after) + len(alias)
    in_specs = in_specs + [pl.BlockSpec(memory_space=pl.ANY)] * extra

    def inner(*refs):
        kernel(*refs[:count], *refs[count + extra :])

    start = count + len(after)
    first_out = len(out_shape) - len(alias)
    operands = (*operands, *after, *alias)
    return pl.pallas_call(
        inner,
        input_output_aliases={start + i: first_out + i for i in range(len(alias))},
        grid_spec=pltpu.PrefetchScalarGridSpec(
            num_scalar_prefetch=1, grid=grid, in_specs=in_specs, out_specs=out_specs, scratch_shapes=scratch
        ),
        out_shape=out_shape,
        compiler_params=params(),
        cost_estimate=pl.CostEstimate(flops=flops, bytes_accessed=moved, transcendentals=0),
        name=name,
    )(place, *operands)


def whole(*shape):
    return pl.BlockSpec(shape, lambda i, p: (0,) * len(shape))


def swap_pairs(size, bit):
    return [(i, i ^ bit) for i in range(size)]


def fast_body(
    tokens,
    time_embedding,
    prefix_length,
    suffix_mask,
    cotangent,
    modulation_weight,
    modulation_bias,
    attention_gain,
    attention_in,
    attention_out,
    feed_gain,
    feed_up,
    feed_up_bias,
    feed_down,
    feed_down_bias,
):
    bf16 = jnp.bfloat16
    f32 = jnp.float32
    _, half, model = tokens.shape
    length = 2 * half
    hidden_width = feed_up.shape[1]
    size = lax.axis_size("dp")
    me = lax.axis_index("seq")
    dp = lax.axis_index("dp")
    place = jnp.stack([dp % 2, me]).astype(jnp.int32)
    swap = swap_pairs(2, 1)
    shape = jax.ShapeDtypeStruct

    def mine(array):
        return lax.dynamic_index_in_dim(array, me, 0, False)

    def theirs(array):
        return lax.dynamic_index_in_dim(array, 1 - me, 0, False)

    other = lax.ppermute(theirs(tokens), "seq", swap)
    positions = me * half + jnp.arange(half, dtype=jnp.int32)
    live = (positions[None, :] >= prefix_length[:, None]) & (suffix_mask == 1)
    live_cot = jnp.where(live[:, :, None], cotangent, jnp.zeros_like(cotangent))
    own_cot = mine(live_cot)
    other_cot = lax.ppermute(theirs(live_cot), "seq", swap)

    modulation = jnp.einsum(
        "c,oc->o", mine(time_embedding), modulation_weight, preferred_element_type=f32
    ) + modulation_bias.astype(f32)
    modulation = modulation.reshape(6, model)
    gain_one = attention_gain.astype(f32)[None]
    gain_two = feed_gain.astype(f32)[None]
    cosine, sines = turn_tables(length)
    table = pl.BlockSpec((None, length, 128), lambda i, p: (p[1], 0, 0))
    own_rows = pl.BlockSpec((None, half, model), lambda i, p: (p[1], 0, 0))
    blocks = half // T_ROWS

    def project(source, spec, start, alias):
        turn = pl.BlockSpec((None, T_ROWS, 128), lambda i, p: (p[1], i + start, 0))
        return call(
            lambda p, *refs: project_kernel(*refs),
            (blocks,),
            place,
            [spec, whole(6, model), whole(1, model), whole(model, 3 * model), turn, turn],
            [
                pl.BlockSpec((model, T_ROWS), lambda i, p: (0, i + start)),
                pl.BlockSpec((T_ROWS, 3 * model), lambda i, p: (i + start, 0)),
            ],
            [shape((model, length), bf16), shape((length, 3 * model), bf16)],
            [],
            (source, modulation, gain_one, attention_in, cosine, sines),
            "project",
            length * model * 3 * model,
            6 * MIB,
            alias=alias,
        )

    kept = project(tokens, pl.BlockSpec((None, T_ROWS, model), lambda i, p: (p[1], i, 0)), 0, ())
    first_t, qkv = project(other, pl.BlockSpec((T_ROWS, model), lambda i, p: (i, 0)), blocks, kept)
    def column(k):
        return pl.BlockSpec((length, 128), lambda h, p: (0, h + k))

    pairs = model // 128
    exps_block = pl.BlockSpec((2, length, length), lambda h, p: (h, 0, 0))
    attended, exps, inverses = call(
        lambda p, *refs: attend_kernel(*refs),
        (pairs,),
        place,
        [column(0), column(pairs), column(2 * pairs)],
        [column(0), exps_block, column(0)],
        [shape((length, model), bf16), shape((HEADS, length, length), bf16), shape((length, model), f32)],
        [],
        (qkv, qkv, qkv),
        "attend",
        16 * length * length * model,
        32 * MIB,
    )

    tiles = 4
    width = hidden_width // tiles
    groups = size // 2
    share_rows = hidden_width // size
    model_rows = model // size
    down_block = pl.BlockSpec((groups // tiles, share_rows, model), lambda j, p: (j, 0, 0))
    up_block = pl.BlockSpec((groups, None, model_rows, width), lambda j, p: (0, j, 0, 0))
    out_block = whole(groups, model_rows, model)
    (
        own_out,
        other_out,
        grad_middle,
        grad_attended,
        mid_rows,
        up_bias_grad,
        down_keep,
        down_send,
        up_keep,
        up_send,
        out_keep,
        out_send,
    ) = call(
        middle_kernel,
        (tiles,),
        place,
        [own_rows] + [whole(half, model)] * 3
        + [
            whole(length, model),
            whole(6, model),
            whole(1, model),
            whole(model, model),
            pl.BlockSpec((model, width), lambda j, p: (0, j)),
            pl.BlockSpec((1, width), lambda j, p: (0, j)),
            pl.BlockSpec((width, model), lambda j, p: (j, 0)),
            whole(1, model),
        ],
        [
            own_rows,
            whole(half, model),
            whole(length, model),
            whole(length, model),
            whole(6, model),
            pl.BlockSpec((1, width), lambda j, p: (0, j)),
            down_block,
            down_block,
            up_block,
            up_block,
            out_block,
            out_block,
        ],
        [shape((2, half, model), bf16), shape((half, model), bf16)]
        + [shape((length, model), f32), shape((length, model), bf16), shape((6, model), f32), shape((1, hidden_width), f32)]
        + [shape((groups, share_rows, model), bf16)] * 2
        + [shape((groups, tiles, model_rows, width), bf16)] * 2
        + [shape((groups, model_rows, model), bf16)] * 2,
        [
            pltpu.VMEM((length, model), f32),
            pltpu.VMEM((model, length), bf16),
            pltpu.VMEM((length, model), bf16),
            pltpu.VMEM((model, length), bf16),
            pltpu.VMEM((length, model), bf16),
            pltpu.VMEM((length, model), f32),
            pltpu.VMEM((length, model), f32),
            pltpu.VMEM((width, length), bf16),
            pltpu.VMEM((length, width), bf16),
        ],
        (
            tokens,
            other,
            own_cot,
            other_cot,
            attended,
            modulation,
            gain_two,
            attention_out,
            feed_up,
            feed_up_bias.astype(f32)[None],
            feed_down,
            feed_down_bias.astype(f32)[None],
        ),
        "middle",
        12 * length * model * hidden_width + 6 * length * model * model,
        36 * MIB,
    )
    got_out = lax.ppermute(other_out, "seq", swap)
    merge = (groups, hidden_width // size, model)

    def near(k):
        return pl.BlockSpec((length, 128), lambda h: (0, jnp.minimum(h, pairs - 1) + k))

    def fixed(*dims):
        return pl.BlockSpec(dims, lambda h: (0,) * len(dims), pipeline_mode=pl.Buffered(1))

    turn = pl.BlockSpec((None, length, 128), lambda h: (lax.axis_index("seq"), 0, 0), pipeline_mode=pl.Buffered(1))
    own_part = pl.BlockSpec((None, half, model), lambda h: (lax.axis_index("seq"), 0, 0), pipeline_mode=pl.Buffered(1))
    anywhere = pl.BlockSpec(memory_space=pl.ANY)
    scratch = [
        pltpu.VMEM((length, length), bf16),
        pltpu.VMEM((length, 128), f32),
        pltpu.VMEM((length, 3 * model), bf16),
        pltpu.VMEM((length, model), bf16),
        pltpu.SemaphoreType.DMA((2, BACK_COPIES + 1)),
        pltpu.SemaphoreType.DMA((4,)),
    ]
    for (_, piece_rows, order), sent in zip(BACK_PIECES, (False,) * 3 + (True,) * 3):
        scratch += piece_scratch(piece_rows, order, model, sent)
    tokens_grad, sums, down_grad, up_grad, out_grad, in_grad = pl.pallas_call(
        back_kernel,
        grid=(pairs + 2,),
        in_specs=[
            near(0),
            near(pairs),
            near(2 * pairs),
            near(0),
            near(0),
            pl.BlockSpec((2, length, length), lambda h: (jnp.minimum(h, pairs - 1), 0, 0)),
            near(0),
            turn,
            turn,
            fixed(model, length),
            fixed(model, 3 * model),
            own_part,
            fixed(half, model),
            pl.BlockSpec((half, model), lambda h: (jnp.where(h > pairs, 0, 1), 0)),
            fixed(6, model),
            fixed(1, model),
        ]
        + [anywhere] * 6,
        out_specs=[
            anywhere,
            fixed(2, model),
            fixed(hidden_width // size, model),
            fixed(model_rows, hidden_width),
            fixed(model_rows, model),
            fixed(model_rows, 3 * model),
        ],
        out_shape=[
            shape((2, half, model), bf16),
            shape((2, model), f32),
            shape((hidden_width // size, model), f32),
            shape((model_rows, hidden_width), f32),
            shape((model_rows, model), f32),
            shape((model_rows, 3 * model), f32),
        ],
        scratch_shapes=scratch,
        compiler_params=pltpu.CompilerParams(vmem_limit_bytes=63 * MIB, collective_id=0, has_side_effects=True),
        cost_estimate=pl.CostEstimate(flops=40 * length * length * model, bytes_accessed=60 * MIB, transcendentals=0),
        name="back",
    )(
        qkv,
        qkv,
        qkv,
        attended,
        grad_attended,
        exps,
        inverses,
        cosine,
        sines,
        first_t,
        attention_in,
        tokens,
        other,
        grad_middle,
        modulation,
        gain_one,
        down_keep,
        down_send,
        up_keep.reshape(merge),
        up_send.reshape(merge),
        out_keep,
        out_send,
    )
    in_rows = [sums[0], sums[1] * gain_one[0], sums[1] * (1.0 + modulation[1])]
    block_output = lax.dynamic_update_index_in_dim(own_out, got_out, 1 - me, 0)

    grad_modulation = jnp.concatenate([in_rows[0], in_rows[1], mid_rows[0:4].reshape(-1)])
    own_time = jnp.einsum("o,oc->c", grad_modulation, modulation_weight.astype(f32), precision=highest)
    got_time = lax.ppermute(own_time, "seq", swap)
    time_grad = jnp.where(me == 0, jnp.stack([own_time, got_time]), jnp.stack([got_time, own_time]))

    vectors = [grad_modulation, in_rows[2], mid_rows[4], up_bias_grad[0], mid_rows[5], mine(time_embedding).astype(f32)]
    vectors = jnp.concatenate(vectors)
    everyone = lax.all_gather(vectors, ("dp", "seq"), axis=0)

    def shard_of(start, width):
        rows = width // size
        return lax.dynamic_slice_in_dim(everyone, start + dp * rows, rows, 1)

    modulation_part = shard_of(0, 6 * model)
    modulation_weight_grad = jnp.einsum("so,sc->oc", modulation_part, everyone[:, 9 * model + hidden_width :], precision=highest)
    starts = (6 * model, 7 * model, 8 * model, 8 * model + hidden_width)
    widths = (model, model, hidden_width, model)
    gain_grad, feed_gain_grad, feed_up_bias_grad, feed_down_bias_grad = [
        jnp.sum(shard_of(a, w), 0) for a, w in zip(starts, widths)
    ]
    return (
        block_output,
        tokens_grad,
        time_grad,
        modulation_weight_grad,
        jnp.sum(modulation_part, 0),
        gain_grad,
        in_grad,
        out_grad,
        feed_gain_grad,
        up_grad,
        feed_up_bias_grad,
        down_grad,
        feed_down_bias_grad,
    )


def body(tokens, *rest):
    sequences, half, model = tokens.shape
    size = lax.axis_size("dp")
    fits = model % (16 * size) == 0 and half % T_ROWS == 0
    fits = fits and size == 16 and lax.axis_size("seq") == 2 and sequences == 2
    return (fast_body if fits else general_body)(tokens, *rest)


def solution(mesh):
    return jax.shard_map(
        body,
        mesh=mesh,
        in_specs=(
            P("dp", "seq", None),
            P("dp", None),
            P("dp"),
            P("dp", "seq"),
            P("dp", "seq", None),
            P(),
            P(),
            P(),
            P(),
            P(),
            P(),
            P(),
            P(),
            P(),
            P(),
        ),
        out_specs=(
            P("dp", "seq", None),
            P("dp", "seq", None),
            P("dp", None),
            P("dp", None),
            P("dp"),
            P("dp"),
            P("dp", None),
            P("dp", None),
            P("dp"),
            P("dp", None),
            P("dp"),
            P("dp", None),
            P("dp"),
        ),
        check_vma=False,
    )
```

profile of v0, /device:TPU:0, one launch (start us, length us, event | category | flops | bytes accessed | tf_op | source)
XLA Modules:
  0.0 306.9 jit_solution(9150214221275907274)
XLA Ops:
  7.2 0.0 all-gather.4.cloned.1.call-start
  7.3 2.2 dynamic-slice_bitcast_fusion.2
  9.4 3.0 collective-permute-start
  12.4 0.1 compare_and_fusion
  12.5 0.2 broadcast_select_fusion
  12.7 0.0 copy-start.8
  12.7 0.0 copy-start.9
  12.8 0.0 copy-start.13
  12.8 1.2 dynamic-slice_bitcast_fusion
  14.0 0.0 collective-permute-start.1
  14.1 0.3 copy-done
  14.3 0.4 convolution_reduce_fusion
  14.8 0.6 reshape.46.refs_2_.refs_6_.mod_ref
  15.4 0.6 broadcast_in_dim.38.refs_3_.gain_ref
  16.0 0.6 reshape.50.refs_7_
  16.6 0.6 broadcast_in_dim.47
  17.2 0.6 reshape.52.refs_12_
  17.8 0.6 pad_add_fusion.refs_0_
  18.4 6.8 %project.2 = (bf16[768,1024]{1,0:T(8,128)(2,1)}, bf16[1024,2304]{1,0:T(8,128)(2,1)}) custom-call(s32[2]{0:T(128)} %pad_add_fusion.refs_0_, bf16[2,512,768]{2,1,0:T(8,128)(2,1)} %own_ref.1, f32[6,768]{1,0:T(8,128)} %reshape.46.refs_2_.refs_6_.mod_ref, f32[1,768]{1,0:T(1,128)} %broadcast_in_dim.38.refs_3_.gain_ref, bf16[768,2304]{1,0:T(8,128)(2,1)} %weight_ref.1, ...), custom_call_target="tpu_custom_call" | custom-call | flops 1811939328 | bytes 6291456 | tf_op jit(solution)/shard_map/project/pallas_call | solution.py:920
  25.2 5.9 %collective-permute-done.refs_1_.refs_2_.other_ref = bf16[512,768]{1,0:T(8,128)(2,1)} collective-permute-done((bf16[512,768]{1,0:T(8,128)(2,1)}, bf16[512,768]{1,0:T(8,128)(2,1)}, u32[]{:S(2)}, u32[]{:S(2)}) %collective-permute-start) | collective-permute-done | bytes 786464 | tf_op jit(solution)/shard_map/ppermute | solution.py:976
  31.1 6.8 %project.3 = (bf16[768,1024]{1,0:T(8,128)(2,1)}, bf16[1024,2304]{1,0:T(8,128)(2,1)}) custom-call(s32[2]{0:T(128)} %pad_add_fusion.refs_0_, bf16[512,768]{1,0:T(8,128)(2,1)} %collective-permute-done.refs_1_.refs_2_.other_ref, f32[6,768]{1,0:T(8,128)} %reshape.46.refs_2_.refs_6_.mod_ref, ...), custom_call_target="tpu_custom_call", output_to_operand_aliasing={{0}: (7, {}), {1}: (8, {})} | custom-call | flops 1811939328 | bytes 6291456 | tf_op jit(solution)/shard_map/project/pallas_call | solution.py:920
  37.9 21.9 %attend.1 = (bf16[1024,768]{1,0:T(8,128)(2,1)}, bf16[12,1024,1024]{2,1,0:T(8,128)(2,1)}, f32[1024,768]{1,0:T(8,128)}) custom-call(s32[2]{0:T(128)} %pad_add_fusion.refs_0_, bf16[1024,2304]{1,0:T(8,128)(2,1)} %get-tuple-element.40.refs_1_.refs_2_.refs_3_.q_ref.k_ref.v_ref, bf16[1024,2304]{1,0:T(8,128)(2,1)} %get-tuple-element.40.refs_1_.refs_2_.refs_3_.q_ref.k_ref.v_ref, ...), custom_call_target="tpu_custom_call" | custom-call | flops 12884901888 | bytes 33554432 | tf_op jit(solution)/shard_map/attend/pallas_call | solution.py:920
  59.9 0.9 copy-done.16
  60.8 59.6 %middle.1 = (bf16[2,512,768]{2,1,0:T(8,128)(2,1)}, bf16[512,768]{1,0:T(8,128)(2,1)}, f32[1024,768]{1,0:T(8,128)}, bf16[1024,768]{1,0:T(8,128)(2,1)}, f32[6,768]{...) custom-call(s32[2]{0:T(128)} %pad_add_fusion.refs_0_, ...), custom_call_target="tpu_custom_call" | custom-call | flops 32614907904 | bytes 37748736 | tf_op jit(solution)/shard_map/middle/pallas_call | solution.py:920
  120.4 0.7 slice.25
  121.1 0.8 slice_reduce_fusion
  122.0 113.0 %back.1 = (bf16[2,512,768]{2,1,0:T(8,128)(2,1)}, f32[2,768]{1,0:T(2,128)}, f32[192,768]{1,0:T(8,128)}, f32[48,3072]{1,0:T(8,128)}, f32[48,768]{1,0:T(8,128)}, /*index=5*/f32[48,2304]{1,0:T(8,128)}) custom-call(bf16[1024,2304]{1,0:T(8,128)(2,1)} %get-tuple-element.40.refs_1_.refs_2_.refs_3_.q_ref.k_ref.v_ref, ...), custom_call_target="tpu_custom_call" | custom-call | flops 32212254720 | bytes 62914560 | tf_op jit(solution)/shard_map/back/pallas_call | solution.py:1141
  235.0 0.8 slice_reduce_fusion.3
  235.9 0.6 reshape.54
  236.5 0.0 all-gather.4.cloned.1.call-update
  236.5 0.1 collective-permute-start.2
  236.7 1.8 fusion.8
  238.5 2.0 collective-permute-start.3
  240.6 15.3 %collective-permute-done.3 = f32[128]{0:T(128)S(1)} collective-permute-done((f32[128]{0:T(128)S(1)}, f32[128]{0:T(128)S(1)}, u32[]{:S(2)}, u32[]{:S(2)}) %collective-permute-start.3) | collective-permute-done | bytes 544 | tf_op jit(solution)/shard_map/ppermute | solution.py:1212
  255.9 0.6 maximum_select_fusion
  256.5 0.9 bitcast_dynamic-update-slice_fusion
  257.4 31.1 %all-gather.4.cloned.1.call-done = f32[32,1,10112]{2,1,0:T(1,128)} async-done(((f32[1,1,10112]{2,1,0:T(1,128)}), f32[32,1,10112]{2,1,0:T(1,128)}) %all-gather.4.cloned.1.call-update) | async-done | bytes 1294352 | tf_op jit(solution)/shard_map/all_gather | solution.py:1217
  288.5 1.4 copy.39
  289.9 1.6 fusion.7
  291.5 1.1 fusion
  292.6 1.5 dynamic-slice_reduce_fusion
  294.1 1.5 dynamic-slice_reduce_fusion.1
  295.6 1.1 copy.56
  296.7 0.1 copy-done.5
  296.9 0.8 copy.57
  297.6 0.7 copy.58
  298.3 0.8 copy.59
  299.1 0.8 copy.60
  (44 shorter events, 0.2 us)
Async XLA Ops:
  7.2 5.2 %copy-start.11 = (s32[2,512]{1,0:T(2,128)S(1)}, s32[2,512]{1,0:T(2,128)}, u32[]{:S(2)}) copy-start(s32[2,512]{1,0:T(2,128)} %param.20) | copy-start | bytes 12292
  7.2 5.2 %copy-start.15 = (s32[2]{0:T(128)S(1)}, s32[2]{0:T(128)}, u32[]{:S(2)}) copy-start(s32[2]{0:T(128)} %param.19) | copy-start | bytes 28
  7.2 5.3 %copy-start.2 = (bf16[2,512,768]{2,1,0:T(8,128)(2,1)S(1)}, bf16[2,512,768]{2,1,0:T(8,128)(2,1)}, u32[]{:S(2)}) copy-start(bf16[2,512,768]{2,1,0:T(8,128)(2,1)} %param.21) | copy-start | bytes 4718596
  7.2 281.3 %all-gather.4.cloned.1.call-start = ((), (), s32[]{:S(2)}) async-start(), calls=%async_computation | async-start | bytes 1334784 | tf_op jit(solution)/shard_map/all_gather | solution.py:1217
  9.4 21.6 %collective-permute-start = (bf16[512,768]{1,0:T(8,128)(2,1)}, bf16[512,768]{1,0:T(8,128)(2,1)}, u32[]{:S(2)}, u32[]{:S(2)}) collective-permute-start(bf16[512,768]{1,0:T(8,128)(2,1)} %dynamic-slice_bitcast_fusion.2), channel_id=1, source_target_pairs={{0,1},{1,0},{2,3},{3,2},{4,5},{5,4},{6,7},{7,6},{8,9},{9,8},{10,11... | collective-permute-start | bytes 2359304 | tf_op jit(solution)/shard_map/ppermute | solution.py:976
  12.7 1.6 copy-start
  12.7 1.6 copy-start.14
  12.7 2.0 copy-start.8
  12.7 2.7 copy-start.9
  12.8 3.3 %copy-start.12 = (bf16[768]{0:T(1024)(128)(2,1)S(1)}, bf16[768]{0:T(1024)(128)(2,1)}, u32[]{:S(2)}) copy-start(bf16[768]{0:T(1024)(128)(2,1)} %param.27) | copy-start | bytes 4612
  12.8 3.8 %copy-start.10 = (bf16[3072]{0:T(1024)(128)(2,1)S(1)}, bf16[3072]{0:T(1024)(128)(2,1)}, u32[]{:S(2)}) copy-start(bf16[3072]{0:T(1024)(128)(2,1)} %param.29) | copy-start | bytes 18436
  12.8 4.4 %copy-start.13 = (bf16[768]{0:T(1024)(128)(2,1)S(1)}, bf16[768]{0:T(1024)(128)(2,1)}, u32[]{:S(2)}) copy-start(bf16[768]{0:T(1024)(128)(2,1)} %param.31) | copy-start | bytes 4612
  14.0 45.8 %collective-permute-start.1 = (bf16[512,768]{1,0:T(8,128)(2,1)}, bf16[512,768]{1,0:T(8,128)(2,1)S(1)}, u32[]{:S(2)}, u32[]{:S(2)}) collective-permute-start(bf16[512,768]{1,0:T(8,128)(2,1)} %get-tuple-element.74), channel_id=1, source_target_pairs={{0,1},{1,0},{2,3},{3,2},{4,5},{5,4},{6,7},{7,6},{8,9},{9,8},{10,11... | collective-permute-start | bytes 2359304 | tf_op jit(solution)/shard_map/ppermute | solution.py:981
  59.9 0.9 copy-start.16
  122.0 113.9 %copy-start.7 = (f32[1,3072]{1,0:T(1,128)S(1)}, f32[1,3072]{1,0:T(1,128)}, u32[]{:S(2)}) copy-start(f32[1,3072]{1,0:T(1,128)} %get-tuple-element.58) | copy-start | bytes 36868
  236.5 19.9 %collective-permute-start.2 = (bf16[512,768]{1,0:T(8,128)(2,1)}, bf16[512,768]{1,0:T(8,128)(2,1)S(1)}, u32[]{:S(2)}, u32[]{:S(2)}) collective-permute-start(bf16[512,768]{1,0:T(8,128)(2,1)} %get-tuple-element.43), channel_id=1, source_target_pairs={{0,1},{1,0},{2,3},{3,2},{4,5},{5,4},{6,7},{7,6},{8,9},{9,8},{10,11... | collective-permute-start | bytes 2359304 | tf_op jit(solution)/shard_map/ppermute | solution.py:1119
  238.5 17.4 %collective-permute-start.3 = (f32[128]{0:T(128)S(1)}, f32[128]{0:T(128)S(1)}, u32[]{:S(2)}, u32[]{:S(2)}) collective-permute-start(f32[128]{0:T(128)S(1)} %bitcast.35), channel_id=1, source_target_pairs={{0,1},{1,0},{2,3},{3,2},{4,5},{5,4},{6,7},{7,6},{8,9},{9,8},{10,11... | collective-permute-start | bytes 1544 | tf_op jit(solution)/shard_map/ppermute | solution.py:1212
  257.4 38.2 %copy-start.1 = (bf16[2,512,768]{2,1,0:T(8,128)(2,1)S(1)}, bf16[2,512,768]{2,1,0:T(8,128)(2,1)}, u32[]{:S(2)}) copy-start(bf16[2,512,768]{2,1,0:T(8,128)(2,1)} %get-tuple-element.90) | copy-start | bytes 4718596
  295.6 1.3 copy-start.5
  295.6 2.0 copy-start.6
  295.6 2.7 copy-start.4
  296.9 2.2 copy-start.3
Sparse Core Ops, SparseCore 0:
  236.7 51.7 all-gather.3
where the time goes:
time: 313 us; the launch traced here: 307 us
  Pallas kernels  208 us (66%)
  waiting for transfers between devices  52.3 us (17%)
  local copies, waits for them, and re-layouts  16.8 us (5%)
  between operations  14.5 us (5%)
  other arithmetic  6.7 us (2%)
  starting transfers between devices  5.13 us (2%)
  matrix products  3.35 us (1%)
    pallas_call x1, Pallas kernels, fast_body(): pl.pallas_call(back_kernel, grid=(pairs + 2,), in_specs=[near(0), near(pa...  113 us
    pallas_call x4, Pallas kernels, call(): pl.pallas_call(inner, input_output_aliases={start + i: first_out + i for...  95.2 us
    all_gather x1, waiting for transfers between devices, fast_body(): everyone = lax.all_gather(vectors, ('dp', 'seq'), axis=0)  31.1 us
    ppermute x1, waiting for transfers between devices, fast_body(): got_time = lax.ppermute(own_time, 'seq', swap)  15.3 us
    unnamed x46, local copies, waits for them, and re-layouts  7.63 us
  transfers between devices with their start and end apart: 5, of which 3 were waited for; matrix products, arithmetic and copies ran while one was open for 3% of the time, Pallas kernels for 12%

commit v1 on v0

--- a/solution.py
+++ b/solution.py
@@ -323,6 +323,8 @@
 
 
 T_ROWS = 256
+MIDDLE_ROWS = 512
+PROJECT_ROWS = 512
 MIB = 1 << 20
 
 
@@ -367,7 +369,7 @@
 
 
 def attend_kernel(q_ref, k_ref, v_ref, out_ref, exp_ref, inv_ref):
-    rows = T_ROWS
+    rows = 128
     length = q_ref.shape[0]
     lane = lax.broadcasted_iota(jnp.int32, (rows, 128), 1)
     keys = k_ref[...]
@@ -398,7 +400,6 @@
 
 
 def middle_kernel(
-    core_ref,
     own_ref,
     other_ref,
     own_cot_ref,
@@ -417,25 +418,127 @@
     grad_attended_ref,
     rows_ref,
     up_bias_grad_ref,
-    down_keep_ref,
-    down_send_ref,
-    up_keep_ref,
-    up_send_ref,
+    down_sum_ref,
+    down_tail_ref,
+    upv_sum_ref,
+    upx_sum_ref,
     out_keep_ref,
     out_send_ref,
-    branch_one,
-    attended_t,
-    second,
     second_t,
     grad_two,
     sum_two,
     sum_second,
     act_t,
-    grad_hidden,
+    down_keep,
+    down_give,
+    down_got,
+    up_keep,
+    up_give,
+    up_got,
+    down_half,
+    down_half_got,
+    down_part,
+    down_part_got,
+    up_part,
+    up_part_got,
+    up_half,
+    up_half_got,
+    sems,
 ):
-    rows = T_ROWS
+    rows = MIDDLE_ROWS
     step = pl.program_id(0)
-    core = core_ref[0]
+    links = Links()
+    core = links.bit["C"]
+    tiles = down_keep.shape[0]
+
+    per_tile = 7
+    last = tiles - 1
+
+    def first_copies(tile):
+        return [
+            remote(give.at[tile], got.at[tile], sems, tile * per_tile + i, links.partner["C"])
+            for i, (give, got) in enumerate(((down_give, down_got), (up_give, up_got)))
+        ]
+
+    def down_copy(tile):
+        return remote(down_half.at[tile], down_half_got.at[tile], sems, tile * per_tile + 2, links.partner["Y"])
+
+    def down_on_copy(tile):
+        return remote(down_part.at[tile], down_part_got.at[tile], sems, tile * per_tile + 3, links.partner["X"])
+
+    def up_copies(tile):
+        return [
+            remote(up_part.at[tile, i], up_part_got.at[tile, i], sems, tile * per_tile + 4 + i, links.partner[flip])
+            for i, flip in enumerate(Z_FLIPS)
+        ]
+
+    def up_last_copy():
+        return remote(up_half, up_half_got, sems, last * per_tile + 4, links.partner["X"])
+
+    def total(*terms):
+        return sum(term.astype(jnp.float32) for term in terms).astype(jnp.bfloat16)
+
+    half_rows = down_half.shape[2]
+    home = pl.ds(pl.multiple_of(links.me * half_rows, 16), half_rows)
+    away = pl.ds(pl.multiple_of((1 - links.me) * half_rows, 16), half_rows)
+    z_at = links.bit["W"] * 2 + links.bit["Z"]
+
+    def flipped(flip):
+        values = {bit: 1 - links.bit[bit] if bit in flip else links.bit[bit] for bit in "WZ"}
+        return values["W"] * 2 + values["Z"]
+
+    def send_on(tile, final):
+        for copy in first_copies(tile):
+            copy.wait_recv()
+        for x in range(2):
+            down_half[tile, x] = total(down_keep[tile, x, away], down_got[tile, x, away])
+        down_copy(tile).start()
+        if final:
+            for z in range(4):
+                other = 2 * z + 1 - links.bit["X"]
+                up_half[z] = total(up_keep[tile, other], up_got[tile, other])
+            up_last_copy().start()
+        else:
+            for i, flip in enumerate(Z_FLIPS):
+                for x in range(2):
+                    other = 2 * flipped(flip) + x
+                    up_part[tile, i, x] = total(up_keep[tile, other], up_got[tile, other])
+            for copy in up_copies(tile):
+                copy.start()
+
+    def send_down(tile):
+        down_copy(tile).wait_recv()
+        x = 1 - links.bit["X"]
+        down_part[tile] = total(down_keep[tile, x, home], down_got[tile, x, home], down_half_got[tile, x])
+        down_on_copy(tile).start()
+
+    def settle(tile, final):
+        if final:
+            down_copy(tile).wait_recv()
+            for x in range(2):
+                down_tail_ref[x] = total(down_keep[tile, x, home], down_got[tile, x, home], down_half_got[tile, x])
+        else:
+            down_on_copy(tile).wait_recv()
+            x = links.bit["X"]
+            terms = (down_keep[tile, x, home], down_got[tile, x, home], down_half_got[tile, x], down_part_got[tile])
+            down_sum_ref[tile] = total(*terms)
+        if final:
+            up_last_copy().wait_recv()
+            for z in range(4):
+                mine = 2 * z + links.bit["X"]
+                upx_sum_ref[z] = total(up_keep[tile, mine], up_got[tile, mine], up_half_got[z])
+        else:
+            for copy in up_copies(tile):
+                copy.wait_recv()
+            for x in range(2):
+                mine = 2 * z_at + x
+                got = [up_part_got[tile, i, x] for i in range(3)]
+                upv_sum_ref[x, tile] = total(up_keep[tile, mine], up_got[tile, mine], *got)
+
+    @pl.when(step == 0)
+    def _():
+        links.greet()
+
     half, model = own_ref.shape
     length = 2 * half
     scaling = gain_ref[...] * (1.0 + mod_ref[4:5])
@@ -453,14 +556,14 @@
         for chunk in range(length // rows):
             at = slice(chunk * rows, (chunk + 1) * rows)
             branch = dot(attended_ref[at], out_weight_ref[...], 1, 0)
-            branch_one[at] = branch
-            attended_t[:, at] = attended_ref[at].T
+            grad_middle_ref[at] = branch
             sum_two[at] = jnp.zeros((rows, model), jnp.float32)
             sum_second[at] = jnp.zeros((rows, model), jnp.float32)
             middle = pick(own_ref, other_ref, chunk).astype(jnp.float32) + gate_one * branch
             normed, _ = norm_rows(middle)
             rounded = (normed * scaling + shift_two).astype(jnp.bfloat16)
-            second[at] = rounded
+            place = (chunk * rows) % half
+            (own_out_ref if chunk * rows < half else other_out_ref)[place : place + rows] = rounded
             second_t[:, at] = rounded.T
             grad = (gate_two * pick(own_cot_ref, other_cot_ref, chunk).astype(jnp.float32)).astype(jnp.bfloat16)
             grad_two[at] = grad
@@ -472,8 +575,18 @@
     width = up.shape[1]
     bias_sum = jnp.zeros((1, width), jnp.float32)
     for chunk in range(length // rows):
+        if chunk * rows == half:
+
+            @pl.when(step > 0)
+            def _():
+                send_on(step - 1, False)
+
+            @pl.when(step > 1)
+            def _():
+                send_down(step - 2)
+
         at = slice(chunk * rows, (chunk + 1) * rows)
-        hidden = dot(second[at], up, 1, 0) + up_bias_ref[...]
+        hidden = dot(pick(own_out_ref, other_out_ref, chunk), up, 1, 0) + up_bias_ref[...]
         squared = hidden * hidden
         tanh = jnp.tanh(hidden * (0.7978845608028654 + 0.035677408136300125 * squared))
         gate = 0.5 + 0.5 * tanh
@@ -481,23 +594,25 @@
         slope = gate + (0.5 * hidden) * (1.0 - tanh * tanh) * (0.7978845608028654 + 0.10703222440890037 * squared)
         act_t[:, at] = activated.T
         grad = (slope * dot(grad_two[at], down, 1, 1)).astype(jnp.bfloat16)
-        grad_hidden[at] = grad
+        grad_attended_ref[at] = grad
         bias_sum = bias_sum + jnp.sum(grad.astype(jnp.float32), 0, keepdims=True)
         sum_two[at] += dot(activated, down, 1, 0)
         sum_second[at] += dot(grad, up, 1, 1)
 
     up_bias_grad_ref[...] = bias_sum
-    down_grad = dot(act_t[...], grad_two[...], 1, 0).astype(jnp.bfloat16).reshape(down_keep_ref.shape[0], 2, -1, model)
-    share(core, (down_grad[:, 0], down_grad[:, 1]), down_keep_ref, down_send_ref, Ellipsis)
-    up_grad = dot(second_t[...], grad_hidden[...], 1, 0).astype(jnp.bfloat16).reshape(up_keep_ref.shape[0], 2, -1, width)
-    share(core, (up_grad[:, 0], up_grad[:, 1]), up_keep_ref, up_send_ref, Ellipsis)
+    down_grad = dot(act_t[...], grad_two[...], 1, 0).astype(jnp.bfloat16).reshape(2, 2, -1, model)
+    share(core, (down_grad[:, 0], down_grad[:, 1]), down_keep, down_give, step)
+    up_grad = dot(second_t[...], grad_attended_ref[...], 1, 0).astype(jnp.bfloat16).reshape(up_keep.shape[1], 2, -1, width)
+    share(core, (up_grad[:, 0], up_grad[:, 1]), up_keep, up_give, step)
+    for copy in first_copies(step):
+        copy.start()
 
     @pl.when(step == pl.num_programs(0) - 1)
     def _():
         sums = [jnp.zeros((1, model), jnp.float32) for _ in range(4)]
         for chunk in range(length // rows):
             at = slice(chunk * rows, (chunk + 1) * rows)
-            branch = branch_one[at]
+            branch = grad_middle_ref[at]
             middle = pick(own_ref, other_ref, chunk).astype(jnp.float32) + gate_one * branch
             normed, inverse = norm_rows(middle)
             branch_two = sum_two[at] + down_bias_ref[...]
@@ -513,17 +628,31 @@
             grad_middle_ref[at] = grad_middle
             grad_one = (gate_one * grad_middle).astype(jnp.bfloat16)
             grad_two[at] = grad_one
+            act_t[:, at] = attended_ref[at].T
             grad_attended_ref[at] = dot(grad_one, out_weight_ref[...], 1, 1).astype(jnp.bfloat16)
             for i, term in enumerate((grad_middle * branch, grad, weighted, cot * branch_two)):
                 sums[i] = sums[i] + jnp.sum(term, 0, keepdims=True)
+            if (chunk + 1) * rows == half:
+                send_on(last, True)
+                send_down(last - 1)
         rows_ref[0:1] = sums[0]
         rows_ref[1:2] = sums[1]
         rows_ref[2:3] = sums[2] * gain_ref[...]
         rows_ref[3:4] = sums[3]
         rows_ref[4:5] = sums[2] * (1.0 + mod_ref[4:5])
-        out_grad = dot(attended_t[...], grad_two[...], 1, 0).astype(jnp.bfloat16)
+        out_grad = dot(act_t[...], grad_two[...], 1, 0).astype(jnp.bfloat16)
         out_grad = out_grad.reshape(out_keep_ref.shape[0], 2, -1, model)
         share(core, (out_grad[:, 0], out_grad[:, 1]), out_keep_ref, out_send_ref, Ellipsis)
+        for tile in range(last):
+            settle(tile, False)
+        settle(last, True)
+        for tile in range(tiles):
+            ups = [up_last_copy()] if tile == last else up_copies(tile)
+            for copy in first_copies(tile) + [down_copy(tile)] + ([] if tile == last else [down_on_copy(tile)]) + ups:
+                copy.wait_send()
+
+
+Z_FLIPS = ("Z", "W", "ZW")
 
 
 class Links:
@@ -531,11 +660,23 @@
         dp = lax.axis_index("dp")
         self.me = lax.axis_index("seq")
         self.bit = {"C": dp % 2, "X": (dp // 2) % 2, "Z": (dp // 4) % 2, "W": (dp // 8) % 2, "Y": self.me}
-        self.partner = {
-            name: (dp + jump * (1 - 2 * self.bit[name]), self.me)
-            for name, jump in (("C", 1), ("X", 2), ("Z", 4), ("W", 8))
-        }
+        jump = {name: size * (1 - 2 * self.bit[name]) for name, size in (("C", 1), ("X", 2), ("Z", 4), ("W", 8))}
+        self.partner = {name: (dp + jump[name], self.me) for name in "CXZW"}
+        self.partner["ZW"] = (dp + jump["Z"] + jump["W"], self.me)
         self.partner["Y"] = (dp, 1 - self.me)
+
+    def place(self):
+        return self.me * 16 + self.bit["X"] * 8 + self.bit["W"] * 4 + self.bit["Z"] * 2 + self.bit["C"]
+
+    def greet(self):
+        barrier = pltpu.get_barrier_semaphore()
+        for device in self.partner.values():
+            pl.semaphore_signal(barrier, inc=1, device_id=device, device_id_type=pl.DeviceIdType.MESH)
+        pl.semaphore_wait(barrier, len(self.partner))
+
+
+def flips_of(kind):
+    return Z_FLIPS if kind == "V" else (kind,)
 
 
 def remote(source, target, sems, slot, device):
@@ -549,60 +690,55 @@
     )
 
 
-def stage_shapes(rows, order):
-    count = 8
-    shapes = []
-    for kind in order:
-        if kind == "Y":
-            rows //= 2
-        else:
-            count //= 2
-        shapes.append((count, rows))
-    shapes.append((1, rows))
-    return shapes
-
-
-def piece_scratch(rows, order, width, sent):
-    shapes = [(8, rows)] * (3 if sent else 2)
-    for shape in stage_shapes(rows, order):
-        shapes += [shape] * 2
-    return [pltpu.VMEM((count, r, width), jnp.bfloat16) for count, r in shapes]
+def piece_scratch(spec):
+    _, rows, width, left, order, kind = spec
+    count = 1 << len(left)
+    shapes = [count] * (1 + ("summed", "given", "made").index(kind))
+    for step in order:
+        count //= 4 if step == "V" else 2
+        shapes += [count * len(flips_of(step))] * 2
+    shapes += [1] * 2
+    return [pltpu.VMEM((c, rows, width), jnp.bfloat16) for c in shapes]
 
 
 class Piece:
-    def __init__(self, links, refs, rows, order, sems, slot, source=None):
+    def __init__(self, links, refs, spec, sems, slot, source=None, split=False):
         refs = list(refs)
+        _, _, _, left, order, kind = spec
         self.links = links
         self.sems = sems
         self.slot = slot
         self.order = list(order)
-        self.rows = rows
-        self.split = False
+        self.split = split
+        self.left = list(left)
         self.keep = refs.pop(0)
-        first = refs.pop(0)
-        self.source = source if source is not None else refs.pop(0)
+        self.terms = [(self.keep, list(self.left))]
+        self.copies = []
+        self.flying = []
+        if kind != "summed":
+            first = refs.pop(0)
+            self.source = refs.pop(0) if kind == "made" else source
+            copy = (self.source, first, sems, slot, links.partner["C"])
+            self.slot += 1
+            self.copies.append(copy)
+            self.flying = [(copy, first, list(self.left))]
         self.buffers = refs
-        self.left = ["W", "Z", "X"]
-        self.terms = [(self.keep, list(self.left), False)]
-        copy = (self.source, first, sems, slot, links.partner["C"])
-        self.slot += 1
-        self.copies = [copy]
-        self.flying = (copy, first, list(self.left), False)
-
-    def launch(self, source, target, kind, bits):
-        copy = (source, target, self.sems, self.slot, self.links.partner[kind])
+
+    def launch(self, source, target, flip):
+        copy = (source, target, self.sems, self.slot, self.links.partner[flip])
         self.slot += 1
         remote(*copy).start()
         self.copies.append(copy)
-        self.flying = (copy, target, list(bits), self.split)
+        self.flying.append((copy, target, list(self.left)))
 
     def begin(self):
         remote(*self.copies[0]).start()
 
     def arrive(self):
-        copy, target, bits, split = self.flying
-        remote(*copy).wait_recv()
-        self.terms.append((target, bits, split))
+        for copy, target, bits in self.flying:
+            remote(*copy).wait_recv()
+            self.terms.append((target, bits))
+        self.flying = []
 
     def index(self, bits, values):
         at = 0
@@ -610,30 +746,25 @@
             at = at * 2 + values[bit]
         return at
 
-    def add(self, out, kind):
+    def add(self, out, flip):
         links = self.links
-        left = [bit for bit in self.left if bit != kind]
         rows = out.shape[1]
         block = 48
-        for combo in range(1 << len(left)):
+        for combo in range(1 << len(self.left)):
             values = dict(links.bit)
-            for place, bit in enumerate(left):
-                values[bit] = (combo >> (len(left) - 1 - place)) & 1
-            if kind is not None and kind != "Y":
-                values[kind] = 1 - links.bit[kind]
-            indices = [self.index(bits, values) for _, bits, _ in self.terms]
+            for bit in flip:
+                values[bit] = 1 - links.bit[bit]
+            for place, bit in enumerate(self.left):
+                values[bit] = (combo >> (len(self.left) - 1 - place)) & 1
+            indices = [self.index(bits, values) for _, bits in self.terms]
 
             def some(i, carry, indices=indices, combo=combo):
-                start = pl.multiple_of(i * block, 16)
+                at = pl.ds(pl.multiple_of(i * block, 16), block)
                 total = None
-                for (ref, _, split), at in zip(self.terms, indices):
-                    begin = start
-                    if not split and (kind == "Y" or self.split):
-                        half = (1 - links.me) if kind == "Y" else links.me
-                        begin = pl.multiple_of(half * rows + i * block, 16)
-                    term = ref[at, pl.ds(begin, block), :].astype(jnp.float32)
+                for (ref, _), index in zip(self.terms, indices):
+                    term = ref[index, at, :].astype(jnp.float32)
                     total = term if total is None else total + term
-                out[combo, pl.ds(start, block), :] = total.astype(jnp.bfloat16)
+                out[combo, at, :] = total.astype(jnp.bfloat16)
                 return carry
 
             lax.fori_loop(0, rows // block, some, 0)
@@ -642,21 +773,22 @@
         self.arrive()
         kind = self.order.pop(0)
         out, target = self.buffers.pop(0), self.buffers.pop(0)
-        self.add(out, kind)
-        if kind == "Y":
-            self.split = True
-        else:
-            self.left.remove(kind)
-        self.launch(out, target, kind, self.left)
+        for bit in "WZ" if kind == "V" else kind:
+            self.left.remove(bit)
+        count = 1 << len(self.left)
+        for i, flip in enumerate(flips_of(kind)):
+            part = pl.ds(i * count, count)
+            self.add(out.at[part], flip)
+            self.launch(out.at[part], target.at[part], flip)
 
     def last(self):
         self.arrive()
         self.total, self.got = self.buffers.pop(0), self.buffers.pop(0)
-        self.add(self.total, None)
-        self.launch(self.total, self.got, "Y", [])
+        self.add(self.total, "")
+        self.launch(self.total, self.got, "Y")
 
     def result(self, store):
-        remote(*self.flying[0]).wait_recv()
+        remote(*self.flying[0][0]).wait_recv()
         rows = self.total.shape[1]
         total = self.total[0].astype(jnp.float32)
         got = self.got[0].astype(jnp.float32)
@@ -667,8 +799,41 @@
             store(slice(0, rows), total + got)
 
 
-BACK_PIECES = (("down", 192, "YXZW"), ("up", 192, "XZW"), ("out", 48, "ZXW"), ("in0", 48, "ZXW"), ("in1", 48, "ZXW"), ("in2", 48, "XZW"))
-BACK_COPIES = sum(2 + len(order) for _, _, order in BACK_PIECES)
+CHUNKS = (3, 2, 1)
+BACK_PIECES = (
+    ("down", 96, 768, "WZ", "V", "summed"),
+    ("upv", 144, 768, "X", "X", "summed"),
+    ("upx", 48, 768, "WZ", "V", "summed"),
+    ("out", 48, 768, "WZX", "XV", "given"),
+    *((f"in{i}", 48, 384 * pairs, "WZX", "XV", "made") for i, pairs in enumerate(CHUNKS)),
+)
+
+
+def copies_of(spec):
+    return sum(len(flips_of(kind)) for kind in spec[4]) + 1 + (spec[5] != "summed")
+
+
+BACK_COPIES = sum(copies_of(spec) for spec in BACK_PIECES)
+HOPS = (("C",), Z_FLIPS, ("X",), ("Y",))
+SPREAD = "XZWCY"
+
+
+def spread_copies(links, array, sems, slot, number):
+    place = links.place()
+    have = (1, 2, 8, 16)[number]
+    part = array.at[pl.ds((place // have) * have, have)]
+    slot += (0, 1, 4, 5)[number]
+    return [remote(part, part, sems, slot + i, links.partner[flip]) for i, flip in enumerate(HOPS[number])]
+
+
+def start_all(copies):
+    for copy in copies:
+        copy.start()
+
+
+def receive_all(copies):
+    for copy in copies:
+        copy.wait_recv()
 
 
 def back_kernel(
@@ -681,29 +846,60 @@
     inv_ref,
     cos_ref,
     sin_ref,
+    first_t_hbm,
+    weight_hbm,
+    own_hbm,
+    other_hbm,
+    grad_middle_hbm,
+    mod_ref,
+    gain_ref,
+    down_keep,
+    down_tail_hbm,
+    upv_keep,
+    upx_keep,
+    out_keep,
+    out_send,
+    mid_rows_ref,
+    up_bias_ref,
+    time_ref,
+    mod_weight_hbm,
+    other_block_ref,
+    _,
+    tokens_grad_ref,
+    time_grad_ref,
+    mod_weight_grad_ref,
+    mod_bias_grad_ref,
+    gain_grad_ref,
+    feed_gain_grad_ref,
+    up_bias_grad_ref,
+    down_bias_grad_ref,
+    down_ref,
+    up_ref,
+    out_grad_ref,
+    in_ref,
+    block_ref,
     first_t_ref,
     weight_ref,
     own_ref,
     other_ref,
     grad_middle_ref,
-    mod_ref,
-    gain_ref,
-    down_keep,
-    down_send,
-    up_keep,
-    up_send,
-    out_keep,
-    out_send,
-    tokens_grad_ref,
-    rows_ref,
-    down_ref,
-    up_ref,
-    out_grad_ref,
-    in_ref,
+    mod_weight_ref,
+    down_tail,
+    down_tail_give,
+    down_tail_got,
     ds_ref,
     dq_sum,
     proj,
     tokens_stage,
+    rows_ref,
+    early,
+    late,
+    running,
+    running_got,
+    by_vector,
+    spread,
+    spread_bias,
+    turned,
     sems,
     local_sems,
     *buffers,
@@ -717,49 +913,125 @@
     pieces = []
     buffers = list(buffers)
     slot = 0
-    sources = [down_send, up_send, out_send, None, None, None]
-    for (_, piece_rows, order), source in zip(BACK_PIECES, sources):
-        count = 2 * len(order) + 4 + (source is None)
-        pieces.append(Piece(links, buffers[:count], piece_rows, order, sems, slot, source))
+    for spec in BACK_PIECES:
+        count = len(piece_scratch(spec))
+        source = out_send if spec[0] == "out" else None
+        pieces.append(Piece(links, buffers[:count], spec, sems, slot, source, spec[0] == "down"))
         buffers = buffers[count:]
-        slot += 2 + len(order)
-    down, up, out, *ins = pieces
-
-    def fetches():
-        pairs = ((down_keep, down), (up_keep, up), (out_keep, out))
-        return [pltpu.make_async_copy(s, p.keep, local_sems.at[i]) for i, (s, p) in enumerate(pairs)]
+        slot += copies_of(spec)
+    down, upv, upx, out, *ins = pieces
+
+    def fetches(first=0, end=11):
+        pairs = (
+            (upv_keep, upv.keep),
+            (down_keep, down.keep.at[pl.ds(0, 3)]),
+            (upx_keep, upx.keep),
+            (out_keep, out.keep),
+            (down_tail_hbm, down_tail),
+            (first_t_hbm, first_t_ref),
+            (weight_hbm, weight_ref),
+            (other_hbm, other_ref),
+            (grad_middle_hbm, grad_middle_ref),
+            (own_hbm.at[links.me], own_ref),
+            (mod_weight_hbm, mod_weight_ref),
+        )
+        return [pltpu.make_async_copy(a, b, local_sems.at[i]) for i, (a, b) in enumerate(pairs) if first <= i < end]
+
+    place = links.place()
+    dp = lax.axis_index("dp")
+    early_slot = BACK_COPIES + 6
+    quarter = half // 4
+    late_slot = early_slot + 6
+    running_slot = late_slot + 6
+    tail_slot = running_slot + 5
+
+    def running_copy(number):
+        partner = links.partner[SPREAD[number]]
+        return remote(running.at[number], running_got.at[number], sems, running_slot + number, partner)
+
+    def tail_copy():
+        return remote(down_tail_give, down_tail_got, sems, tail_slot, links.partner["X"])
+
+    def block_copy(number):
+        at = pl.ds(number * quarter, quarter)
+        target = block_ref.at[links.me, at]
+        return remote(other_block_ref.at[at], target, sems, BACK_COPIES + number, links.partner["Y"])
+
+    def halves(target, at, first, values):
+        middle = model // 2
+        target[at, first : first + 1] = values[:, :middle]
+        target[at, first + 1 : first + 2] = values[:, middle:]
 
     @pl.when(step == 0)
     def _():
-        barrier = pltpu.get_barrier_semaphore()
-        for name in "CXZWY":
-            pl.semaphore_signal(
-                barrier, inc=1, device_id=links.partner[name], device_id_type=pl.DeviceIdType.MESH
-            )
-        pl.semaphore_wait(barrier, 5)
-        for piece in (down, up, out):
-            piece.begin()
+        links.greet()
         for copy in fetches():
             copy.start()
+        out.begin()
+        for m in range(4):
+            halves(early, place, 2 * m, mid_rows_ref[m : m + 1])
+        running[0, 0:2] = mid_rows_ref[4:6]
+        for tile in range(up_bias_ref.shape[1] // model):
+            running[0, 2 + tile : 3 + tile] = up_bias_ref[:, tile * model : (tile + 1) * model]
+        running[0, 6:8] = jnp.zeros((2, model), jnp.float32)
+        start_all(spread_copies(links, early, sems, early_slot, 0))
+        running_copy(0).start()
+
+    for number in range(1, 6):
+
+        @pl.when(step == number)
+        def _(number=number):
+            if number < 5:
+                receive_all(spread_copies(links, early, sems, early_slot, number - 1))
+                if number < 4:
+                    start_all(spread_copies(links, early, sems, early_slot, number))
+            running_copy(number - 1).wait_recv()
+            running[number] = running[number - 1] + running_got[number - 1]
+            if number < 5:
+                running_copy(number).start()
+                block_copy(number - 1).start()
 
     def at_step(number):
         return pl.when(step == number)
 
-    @at_step(2)
-    def _():
-        for copy in fetches():
-            copy.wait()
-        down.step()
-        up.step()
-        out.step()
-
-    @at_step(3)
-    def _():
-        ins[0].step()
-
-    @at_step(5)
-    def _():
-        ins[1].step()
+    def between():
+        @at_step(0)
+        def _():
+            for copy in fetches(0, 5):
+                copy.wait()
+            down_tail_give[...] = down_tail[1 - links.bit["X"]]
+            tail_copy().start()
+            upv.step()
+            upx.step()
+
+        @at_step(1)
+        def _():
+            tail_copy().wait_recv()
+            kept = down_tail[links.bit["X"]].astype(jnp.float32) + down_tail_got[...].astype(jnp.float32)
+            down.keep[3] = kept.astype(jnp.bfloat16)
+            down.step()
+            out.step()
+
+        @at_step(2)
+        def _():
+            for copy in fetches(5):
+                copy.wait()
+            upx.last()
+            upv.last()
+
+        @at_step(3)
+        def _():
+            ins[0].step()
+
+        @at_step(4)
+        def _():
+            out.step()
+            down.last()
+
+        @at_step(5)
+        def _():
+            ins[1].step()
+            ins[0].step()
 
     lane = lax.broadcasted_iota(jnp.int32, (rows, 128), 1)
 
@@ -775,6 +1047,8 @@
         grad_k = []
         grad_v = []
         for head in range(2):
+            if head == 1:
+                between()
             for chunk in range(length // rows):
                 at = slice(chunk * rows, (chunk + 1) * rows)
                 mask = (lane < 64) == (head == 0)
@@ -800,75 +1074,134 @@
                 turned = piece * cos_ref[at] - swap_halves(piece, lane) * sin_ref[at]
                 proj[at, columns[part]] = turned.astype(jnp.bfloat16)
 
+    starts = [128 * sum(CHUNKS[:i]) for i in range(len(CHUNKS))]
+
     def weight_part(group):
         piece = ins[group]
-        span = model // 3
+        span = 128 * CHUNKS[group]
         for part in range(3):
-            column = part * model + group * span
+            column = part * model + starts[group]
             grad = dot(first_t_ref[...], proj[:, column : column + span], 1, 0).astype(jnp.bfloat16)
             grad = grad.reshape(8, 2, -1, span)
             share(core, (grad[:, 0], grad[:, 1]), piece.keep, piece.source, Ellipsis, slice(part * span, (part + 1) * span))
         piece.begin()
 
-    for group in range(3):
-        at_step(2 * group + 1)(functools.partial(weight_part, group))
+    for group, number in enumerate((2, 4, 5)):
+        at_step(number)(functools.partial(weight_part, group))
 
     scaling = gain_ref[...] * (1.0 + mod_ref[1:2])
 
-    def entry(values_ref, base):
-        sums = [jnp.zeros((1, model), jnp.float32) for _ in range(2)]
-        for chunk in range(half // rows):
-            at = slice(base + chunk * rows, base + (chunk + 1) * rows)
-            local = slice(chunk * rows, (chunk + 1) * rows)
-            grad = dot(proj[at], weight_ref[...], 1, 1)
-            normed, inverse = norm_rows(values_ref[local].astype(jnp.float32))
-            weighted = grad * normed
-            scaled = grad * scaling
-            inner = jnp.mean(weighted * scaling, -1, keepdims=True)
-            result = grad_middle_ref[local] + (scaled - jnp.mean(scaled, -1, keepdims=True) - normed * inner) * inverse
-            tokens_stage[at] = result.astype(jnp.bfloat16)
-            for i, term in enumerate((grad, weighted)):
-                sums[i] = sums[i] + jnp.sum(term, 0, keepdims=True)
-        return jnp.concatenate(sums, 0)
-
-    def away():
-        target = tokens_grad_ref.at[links.me]
-        return remote(tokens_stage.at[pl.ds(half, half)], target, sems, BACK_COPIES, links.partner["Y"])
+    def entry(values_ref, base, chunk):
+        at = slice(base + chunk * rows, base + (chunk + 1) * rows)
+        local = slice(chunk * rows, (chunk + 1) * rows)
+        grad = dot(proj[at], weight_ref[...], 1, 1)
+        normed, inverse = norm_rows(values_ref[local].astype(jnp.float32))
+        weighted = grad * normed
+        scaled = grad * scaling
+        inner = jnp.mean(weighted * scaling, -1, keepdims=True)
+        result = grad_middle_ref[at] + (scaled - jnp.mean(scaled, -1, keepdims=True) - normed * inner) * inverse
+        tokens_stage[at] = result.astype(jnp.bfloat16)
+        return jnp.concatenate([jnp.sum(grad, 0, keepdims=True), jnp.sum(weighted, 0, keepdims=True)], 0)
+
+    def away(chunk):
+        source = tokens_stage.at[pl.ds(half + chunk * rows, rows)]
+        target = tokens_grad_ref.at[links.me, pl.ds(chunk * rows, rows)]
+        return remote(source, target, sems, BACK_COPIES + 4 + chunk, links.partner["Y"])
 
     def home():
-        return pltpu.make_async_copy(tokens_stage.at[pl.ds(0, half)], tokens_grad_ref.at[links.me], local_sems.at[3])
+        return pltpu.make_async_copy(tokens_stage.at[pl.ds(0, half)], tokens_grad_ref.at[links.me], local_sems.at[11])
+
+    def vectors():
+        middle = model // 2
+        for m in range(6):
+            source, row = (late, 2 * m) if m < 2 else (early, 2 * m - 4)
+            by_vector[m, :, 0:middle] = source[:, row, :]
+            by_vector[m, :, middle:model] = source[:, row + 1, :]
+        ones = jnp.ones((32, 128), jnp.float32)
+        factors = jnp.concatenate([late[:, 6, 0:128], ones], 1)
+        unit = mod_weight_grad_ref.shape[0] // 6
+        for part in range(6):
+            at = dp * 6 + part
+            product = lax.dot_general(
+                by_vector[at // 16],
+                factors,
+                (((0,), (0,)), ((), ())),
+                precision=highest,
+                preferred_element_type=jnp.float32,
+            )
+            spread[...] = product
+            kept = spread[pl.ds(pl.multiple_of((at % 16) * unit, 8), unit), :]
+            mod_weight_grad_ref[part * unit : (part + 1) * unit] = kept[:, 0:128]
+            spread_bias[part * unit : (part + 1) * unit] = kept[:, 128:256]
+        mod_bias_grad_ref[...] = spread_bias[...].T[0:1]
+        base = place % 16
+        both = jnp.zeros((2, 128), jnp.float32)
+        for m in range(6):
+            rest = jnp.concatenate([by_vector[m, pl.ds(base, 1)], by_vector[m, pl.ds(base + 16, 1)]], 0)
+            for _ in range(3):
+                high = rest.astype(jnp.bfloat16)
+                both = both + dot(high, mod_weight_ref[m * model : (m + 1) * model], 1, 0)
+                rest = rest - high.astype(jnp.float32)
+        time_grad_ref[...] = both
+        gains = [jnp.sum(late[:, row, :], 0, keepdims=True) for row in (4, 5)]
+        gains = jnp.concatenate(gains, 1)
+        turned[...] = jnp.concatenate([running[5, 0:6], gains, gains], 0).T
+        narrow = turned[pl.ds(pl.multiple_of(dp * unit, 8), unit), :].T
+        feed_gain_grad_ref[...] = narrow[0:1]
+        down_bias_grad_ref[...] = narrow[1:2]
+        gain_grad_ref[...] = narrow[6:7]
+        wide_rows = up_bias_grad_ref.shape[1]
+        share_of = model // wide_rows
+        wide = turned[pl.ds(pl.multiple_of((dp % share_of) * wide_rows, 8), wide_rows), :].T
+        picked = jnp.zeros((1, wide_rows), jnp.float32)
+        for tile in range(4):
+            picked = jnp.where(dp // share_of == tile, wide[2 + tile : 3 + tile], picked)
+        up_bias_grad_ref[...] = picked
 
     @at_step(6)
     def _():
-        rows_ref[...] = entry(other_ref, half)
-        away().start()
+        rows_ref[...] = entry(other_ref, half, 0)
         ins[2].step()
-        ins[0].step()
+        away(0).start()
+        rows_ref[...] += entry(other_ref, half, 1)
+        out.last()
+        away(1).start()
         ins[1].step()
-        out.step()
 
     @at_step(7)
     def _():
-        rows_ref[...] += entry(own_ref, 0)
+        rows_ref[...] += entry(own_ref, 0, 0)
+        ins[2].step()
+        rows_ref[...] += entry(own_ref, 0, 1)
         home().start()
-        down.step()
-        up.step()
-        for piece in (ins[0], out, ins[1], ins[2]):
-            piece.step()
-        down.step()
-        for piece in (ins[0], out, ins[1]):
-            piece.last()
-        up.step()
-        ins[2].step()
-        down.step()
+        scaling_one = 1.0 + mod_ref[1:2]
+        halves(late, place, 0, rows_ref[0:1])
+        halves(late, place, 2, rows_ref[1:2] * gain_ref[...])
+        halves(late, place, 4, rows_ref[1:2] * scaling_one)
+        embedding = time_ref[...].astype(jnp.float32)
+        late[place, 6:7, 0:128] = jnp.where(links.me == 0, embedding[0:1], embedding[1:2])
+        start_all(spread_copies(links, late, sems, late_slot, 0))
+        hop = iter(range(4))
+
+        def hop_on():
+            number = next(hop)
+            receive_all(spread_copies(links, late, sems, late_slot, number))
+            if number < 3:
+                start_all(spread_copies(links, late, sems, late_slot, number + 1))
+
+        ins[0].last()
+        hop_on()
+        ins[1].last()
+        hop_on()
         ins[2].last()
-        down.last()
-        up.last()
-        span = model // 3
+        hop_on()
+        hop_on()
+        vectors()
         for group in range(3):
             def store(at, value, group=group):
+                span = 128 * CHUNKS[group]
                 for part in range(3):
-                    column = part * model + group * span
+                    column = part * model + starts[group]
                     in_ref[at, column : column + span] = value[:, part * span : (part + 1) * span]
 
             ins[group].result(store)
@@ -883,17 +1216,37 @@
 
         down.result(store_down)
 
-        def store_up(at, value):
-            count = up_ref.shape[0]
-            for tile in range(up_ref.shape[1] // model):
-                up_ref[:, tile * model : (tile + 1) * model] = value[tile * count : (tile + 1) * count]
-
-        up.result(store_up)
+        def store_up(first):
+            def store(at, value):
+                count = up_ref.shape[0]
+                for tile in range(value.shape[0] // count):
+                    columns = slice((first + tile) * model, (first + tile + 1) * model)
+                    up_ref[:, columns] = value[tile * count : (tile + 1) * count]
+
+            return store
+
+        upv.result(store_up(0))
+        upx.result(store_up(3))
         home().wait()
-        away().wait()
+        for chunk in range(half // rows):
+            away(chunk).wait()
+        for number in range(4):
+            block_copy(number).wait()
+        for number in range(4):
+            for copy in spread_copies(links, early, sems, early_slot, number) + spread_copies(links, late, sems, late_slot, number):
+                copy.wait_send()
+        for number in range(5):
+            running_copy(number).wait_send()
+        tail_copy().wait_send()
         for piece in pieces:
             for copy in piece.copies:
                 remote(*copy).wait_send()
+
+
+def close_kernel(*refs):
+    count = len(refs) // 2
+    for source, target in zip(refs[:count], refs[count:]):
+        target[...] = source[...]
 
 
 def turn_tables(length):
@@ -989,18 +1342,18 @@
     cosine, sines = turn_tables(length)
     table = pl.BlockSpec((None, length, 128), lambda i, p: (p[1], 0, 0))
     own_rows = pl.BlockSpec((None, half, model), lambda i, p: (p[1], 0, 0))
-    blocks = half // T_ROWS
+    blocks = half // PROJECT_ROWS
 
     def project(source, spec, start, alias):
-        turn = pl.BlockSpec((None, T_ROWS, 128), lambda i, p: (p[1], i + start, 0))
+        turn = pl.BlockSpec((None, PROJECT_ROWS, 128), lambda i, p: (p[1], i + start, 0))
         return call(
             lambda p, *refs: project_kernel(*refs),
             (blocks,),
             place,
             [spec, whole(6, model), whole(1, model), whole(model, 3 * model), turn, turn],
             [
-                pl.BlockSpec((model, T_ROWS), lambda i, p: (0, i + start)),
-                pl.BlockSpec((T_ROWS, 3 * model), lambda i, p: (i + start, 0)),
+                pl.BlockSpec((model, PROJECT_ROWS), lambda i, p: (0, i + start)),
+                pl.BlockSpec((PROJECT_ROWS, 3 * model), lambda i, p: (i + start, 0)),
             ],
             [shape((model, length), bf16), shape((length, 3 * model), bf16)],
             [],
@@ -1011,8 +1364,8 @@
             alias=alias,
         )
 
-    kept = project(tokens, pl.BlockSpec((None, T_ROWS, model), lambda i, p: (p[1], i, 0)), 0, ())
-    first_t, qkv = project(other, pl.BlockSpec((T_ROWS, model), lambda i, p: (i, 0)), blocks, kept)
+    kept = project(tokens, pl.BlockSpec((None, PROJECT_ROWS, model), lambda i, p: (p[1], i, 0)), 0, ())
+    first_t, qkv = project(other, pl.BlockSpec((PROJECT_ROWS, model), lambda i, p: (i, 0)), blocks, kept)
     def column(k):
         return pl.BlockSpec((length, 128), lambda h, p: (0, h + k))
 
@@ -1037,9 +1390,15 @@
     groups = size // 2
     share_rows = hidden_width // size
     model_rows = model // size
-    down_block = pl.BlockSpec((groups // tiles, share_rows, model), lambda j, p: (j, 0, 0))
-    up_block = pl.BlockSpec((groups, None, model_rows, width), lambda j, p: (0, j, 0, 0))
-    out_block = whole(groups, model_rows, model)
+    anywhere = pl.BlockSpec(memory_space=pl.ANY)
+
+    def fixed(*dims):
+        return pl.BlockSpec(dims, lambda h: (0,) * len(dims), pipeline_mode=pl.Buffered(1))
+
+    own_part = pl.BlockSpec((None, half, model), lambda h: (lax.axis_index("seq"), 0, 0), pipeline_mode=pl.Buffered(1))
+    up_tile = pl.BlockSpec((model, width), lambda j: (0, j))
+    bias_tile = pl.BlockSpec((1, width), lambda j: (0, j))
+    down_tile = pl.BlockSpec((width, model), lambda j: (j, 0))
     (
         own_out,
         other_out,
@@ -1047,98 +1406,121 @@
         grad_attended,
         mid_rows,
         up_bias_grad,
-        down_keep,
-        down_send,
-        up_keep,
-        up_send,
+        down_sum,
+        down_tail,
+        upv_sum,
+        upx_sum,
         out_keep,
         out_send,
-    ) = call(
+    ) = pl.pallas_call(
         middle_kernel,
-        (tiles,),
-        place,
-        [own_rows] + [whole(half, model)] * 3
+        grid=(tiles,),
+        in_specs=[own_part]
+        + [fixed(half, model)] * 3
         + [
-            whole(length, model),
-            whole(6, model),
-            whole(1, model),
-            whole(model, model),
-            pl.BlockSpec((model, width), lambda j, p: (0, j)),
-            pl.BlockSpec((1, width), lambda j, p: (0, j)),
-            pl.BlockSpec((width, model), lambda j, p: (j, 0)),
-            whole(1, model),
+            fixed(length, model),
+            fixed(6, model),
+            fixed(1, model),
+            fixed(model, model),
+            up_tile,
+            bias_tile,
+            down_tile,
+            fixed(1, model),
         ],
-        [
-            own_rows,
-            whole(half, model),
-            whole(length, model),
-            whole(length, model),
-            whole(6, model),
-            pl.BlockSpec((1, width), lambda j, p: (0, j)),
-            down_block,
-            down_block,
-            up_block,
-            up_block,
-            out_block,
-            out_block,
+        out_specs=[
+            own_part,
+            fixed(half, model),
+            fixed(length, model),
+            fixed(length, model),
+            fixed(6, model),
+            bias_tile,
+            fixed(tiles - 1, share_rows // 2, model),
+            fixed(2, share_rows // 2, model),
+            fixed(2, tiles - 1, model_rows, model),
+            fixed(4, model_rows, model),
+            fixed(groups, model_rows, model),
+            fixed(groups, model_rows, model),
         ],
-        [shape((2, half, model), bf16), shape((half, model), bf16)]
+        out_shape=[shape((2, half, model), bf16), shape((half, model), bf16)]
         + [shape((length, model), f32), shape((length, model), bf16), shape((6, model), f32), shape((1, hidden_width), f32)]
-        + [shape((groups, share_rows, model), bf16)] * 2
-        + [shape((groups, tiles, model_rows, width), bf16)] * 2
+        + [shape((tiles - 1, share_rows // 2, model), bf16), shape((2, share_rows // 2, model), bf16), shape((2, tiles - 1, model_rows, model), bf16)]
+        + [shape((4, model_rows, model), bf16)]
         + [shape((groups, model_rows, model), bf16)] * 2,
-        [
-            pltpu.VMEM((length, model), f32),
-            pltpu.VMEM((model, length), bf16),
-            pltpu.VMEM((length, model), bf16),
+        scratch_shapes=[
             pltpu.VMEM((model, length), bf16),
             pltpu.VMEM((length, model), bf16),
             pltpu.VMEM((length, model), f32),
             pltpu.VMEM((length, model), f32),
             pltpu.VMEM((width, length), bf16),
-            pltpu.VMEM((length, width), bf16),
-        ],
-        (
-            tokens,
-            other,
-            own_cot,
-            other_cot,
-            attended,
-            modulation,
-            gain_two,
-            attention_out,
-            feed_up,
-            feed_up_bias.astype(f32)[None],
-            feed_down,
-            feed_down_bias.astype(f32)[None],
+        ]
+        + [pltpu.VMEM((tiles, groups // tiles, share_rows, model), bf16)] * 3
+        + [pltpu.VMEM((tiles, groups, model_rows, model), bf16)] * 3
+        + [pltpu.VMEM((tiles, groups // tiles, share_rows // 2, model), bf16)] * 2
+        + [pltpu.VMEM((tiles - 1, share_rows // 2, model), bf16)] * 2
+        + [pltpu.VMEM((tiles - 1, 3, 2, model_rows, model), bf16)] * 2
+        + [pltpu.VMEM((4, model_rows, model), bf16)] * 2
+        + [pltpu.SemaphoreType.DMA((2, 7 * tiles))],
+        compiler_params=pltpu.CompilerParams(vmem_limit_bytes=63 * MIB, collective_id=1, has_side_effects=True),
+        cost_estimate=pl.CostEstimate(
+            flops=12 * length * model * hidden_width + 6 * length * model * model, bytes_accessed=36 * MIB, transcendentals=0
         ),
-        "middle",
-        12 * length * model * hidden_width + 6 * length * model * model,
-        36 * MIB,
-    )
-    got_out = lax.ppermute(other_out, "seq", swap)
-    merge = (groups, hidden_width // size, model)
+        name="middle",
+    )(
+        tokens,
+        other,
+        own_cot,
+        other_cot,
+        attended,
+        modulation,
+        gain_two,
+        attention_out,
+        feed_up,
+        feed_up_bias.astype(f32)[None],
+        feed_down,
+        feed_down_bias.astype(f32)[None],
+    )
+    merge = (2, (tiles - 1) * model_rows, model)
 
     def near(k):
         return pl.BlockSpec((length, 128), lambda h: (0, jnp.minimum(h, pairs - 1) + k))
 
-    def fixed(*dims):
-        return pl.BlockSpec(dims, lambda h: (0,) * len(dims), pipeline_mode=pl.Buffered(1))
-
     turn = pl.BlockSpec((None, length, 128), lambda h: (lax.axis_index("seq"), 0, 0), pipeline_mode=pl.Buffered(1))
-    own_part = pl.BlockSpec((None, half, model), lambda h: (lax.axis_index("seq"), 0, 0), pipeline_mode=pl.Buffered(1))
-    anywhere = pl.BlockSpec(memory_space=pl.ANY)
     scratch = [
+        pltpu.VMEM((model, length), bf16),
+        pltpu.VMEM((model, 3 * model), bf16),
+        pltpu.VMEM((half, model), bf16),
+        pltpu.VMEM((half, model), bf16),
+        pltpu.VMEM((length, model), f32),
+        pltpu.VMEM((6 * model, 128), bf16),
+        pltpu.VMEM((2, share_rows // 2, model), bf16),
+        pltpu.VMEM((share_rows // 2, model), bf16),
+        pltpu.VMEM((share_rows // 2, model), bf16),
         pltpu.VMEM((length, length), bf16),
         pltpu.VMEM((length, 128), f32),
         pltpu.VMEM((length, 3 * model), bf16),
         pltpu.VMEM((length, model), bf16),
-        pltpu.SemaphoreType.DMA((2, BACK_COPIES + 1)),
-        pltpu.SemaphoreType.DMA((4,)),
+        pltpu.VMEM((2, model), f32),
+        pltpu.VMEM((2 * size, 8, model // 2), f32),
+        pltpu.VMEM((2 * size, 8, model // 2), f32),
+        pltpu.VMEM((6, 8, model), f32),
+        pltpu.VMEM((5, 8, model), f32),
+        pltpu.VMEM((6, 2 * size, model), f32),
+        pltpu.VMEM((model, 256), f32),
+        pltpu.VMEM((6 * model_rows, 128), f32),
+        pltpu.VMEM((model, 8), f32),
+        pltpu.SemaphoreType.DMA((2, BACK_COPIES + 24)),
+        pltpu.SemaphoreType.DMA((12,)),
     ]
-    for (_, piece_rows, order), sent in zip(BACK_PIECES, (False,) * 3 + (True,) * 3):
-        scratch += piece_scratch(piece_rows, order, model, sent)
-    tokens_grad, sums, down_grad, up_grad, out_grad, in_grad = pl.pallas_call(
+    for spec in BACK_PIECES:
+        scratch += piece_scratch(spec)
+    def cut(dims):
+        if len(dims) == 3:
+            return pl.BlockSpec((1, *dims[1:]), lambda i: (i, 0, 0))
+        if dims[0] % 16:
+            return pl.BlockSpec(dims, lambda i: (0, 0))
+        return pl.BlockSpec((dims[0] // 2, dims[1]), lambda i: (i, 0))
+
+    results = pl.pallas_call(
         back_kernel,
         grid=(pairs + 2,),
         in_specs=[
@@ -1151,31 +1533,43 @@
             near(0),
             turn,
             turn,
-            fixed(model, length),
-            fixed(model, 3 * model),
-            own_part,
-            fixed(half, model),
-            pl.BlockSpec((half, model), lambda h: (jnp.where(h > pairs, 0, 1), 0)),
+            *[anywhere] * 5,
             fixed(6, model),
             fixed(1, model),
         ]
-        + [anywhere] * 6,
+        + [anywhere] * 6
+        + [fixed(6, model), fixed(1, hidden_width), fixed(2, 128), anywhere, anywhere, anywhere],
         out_specs=[
             anywhere,
-            fixed(2, model),
+            fixed(2, 128),
+            fixed(6 * model_rows, 128),
+            fixed(1, 6 * model_rows),
+            fixed(1, model_rows),
+            fixed(1, model_rows),
+            fixed(1, hidden_width // size),
+            fixed(1, model_rows),
             fixed(hidden_width // size, model),
             fixed(model_rows, hidden_width),
             fixed(model_rows, model),
             fixed(model_rows, 3 * model),
+            anywhere,
         ],
         out_shape=[
             shape((2, half, model), bf16),
-            shape((2, model), f32),
+            shape((2, 128), f32),
+            shape((6 * model_rows, 128), f32),
+            shape((1, 6 * model_rows), f32),
+            shape((1, model_rows), f32),
+            shape((1, model_rows), f32),
+            shape((1, hidden_width // size), f32),
+            shape((1, model_rows), f32),
             shape((hidden_width // size, model), f32),
             shape((model_rows, hidden_width), f32),
             shape((model_rows, model), f32),
             shape((model_rows, 3 * model), f32),
+            shape((2, half, model), bf16),
         ],
+        input_output_aliases={27: 12},
         scratch_shapes=scratch,
         compiler_params=pltpu.CompilerParams(vmem_limit_bytes=63 * MIB, collective_id=0, has_side_effects=True),
         cost_estimate=pl.CostEstimate(flops=40 * length * length * model, bytes_accessed=60 * MIB, transcendentals=0),
@@ -1197,50 +1591,56 @@
         grad_middle,
         modulation,
         gain_one,
-        down_keep,
-        down_send,
-        up_keep.reshape(merge),
-        up_send.reshape(merge),
+        down_sum,
+        down_tail,
+        upv_sum.reshape(merge),
+        upx_sum,
         out_keep,
         out_send,
-    )
-    in_rows = [sums[0], sums[1] * gain_one[0], sums[1] * (1.0 + modulation[1])]
-    block_output = lax.dynamic_update_index_in_dim(own_out, got_out, 1 - me, 0)
-
-    grad_modulation = jnp.concatenate([in_rows[0], in_rows[1], mid_rows[0:4].reshape(-1)])
-    own_time = jnp.einsum("o,oc->c", grad_modulation, modulation_weight.astype(f32), precision=highest)
-    got_time = lax.ppermute(own_time, "seq", swap)
-    time_grad = jnp.where(me == 0, jnp.stack([own_time, got_time]), jnp.stack([got_time, own_time]))
-
-    vectors = [grad_modulation, in_rows[2], mid_rows[4], up_bias_grad[0], mid_rows[5], mine(time_embedding).astype(f32)]
-    vectors = jnp.concatenate(vectors)
-    everyone = lax.all_gather(vectors, ("dp", "seq"), axis=0)
-
-    def shard_of(start, width):
-        rows = width // size
-        return lax.dynamic_slice_in_dim(everyone, start + dp * rows, rows, 1)
-
-    modulation_part = shard_of(0, 6 * model)
-    modulation_weight_grad = jnp.einsum("so,sc->oc", modulation_part, everyone[:, 9 * model + hidden_width :], precision=highest)
-    starts = (6 * model, 7 * model, 8 * model, 8 * model + hidden_width)
-    widths = (model, model, hidden_width, model)
-    gain_grad, feed_gain_grad, feed_up_bias_grad, feed_down_bias_grad = [
-        jnp.sum(shard_of(a, w), 0) for a, w in zip(starts, widths)
-    ]
+        mid_rows,
+        up_bias_grad,
+        time_embedding,
+        modulation_weight,
+        other_out,
+        own_out,
+    )
+    (
+        tokens_grad,
+        time_grad,
+        modulation_weight_grad,
+        modulation_bias_grad,
+        gain_grad,
+        feed_gain_grad,
+        feed_up_bias_grad,
+        feed_down_bias_grad,
+        down_grad,
+        up_grad,
+        out_grad,
+        in_grad,
+        block_output,
+    ) = pl.pallas_call(
+        close_kernel,
+        grid=(2,),
+        in_specs=[cut(r.shape) for r in results],
+        out_specs=[cut(r.shape) for r in results],
+        out_shape=[shape(r.shape, r.dtype) for r in results],
+        compiler_params=params(62),
+        name="close",
+    )(*results)
     return (
         block_output,
         tokens_grad,
         time_grad,
         modulation_weight_grad,
-        jnp.sum(modulation_part, 0),
-        gain_grad,
+        modulation_bias_grad[0],
+        gain_grad[0],
         in_grad,
         out_grad,
-        feed_gain_grad,
+        feed_gain_grad[0],
         up_grad,
-        feed_up_bias_grad,
+        feed_up_bias_grad[0],
         down_grad,
-        feed_down_bias_grad,
+        feed_down_bias_grad[0],
     )
 
 
@@ -1248,7 +1648,7 @@
     sequences, half, model = tokens.shape
     size = lax.axis_size("dp")
     fits = model % (16 * size) == 0 and half % T_ROWS == 0
-    fits = fits and size == 16 and lax.axis_size("seq") == 2 and sequences == 2
+    fits = fits and tokens.shape[1] % PROJECT_ROWS == 0 and rest[10].shape[1] == 4 * model and size == 16 and lax.axis_size("seq") == 2 and sequences == 2
     return (fast_body if fits else general_body)(tokens, *rest)
 
 

time: 313 us -> 224 us (0.72); the launches traced: 307 us -> 223 us
  waiting for transfers between devices: 52.3 us -> 5.55 us
  between operations: 14.5 us -> 0.99 us
  local copies, waits for them, and re-layouts: 16.8 us -> 5.87 us
  Pallas kernels: 208 us -> 204 us
  other arithmetic: 6.7 us -> 2.7 us
    pallas_call x0 -> x2, Pallas kernels: none -> 68.8 us  [the longest x1 64.6 us: fast_body(): pl.pallas_call(middle_kernel, grid=(tiles,), in_specs=[own_part] + [fixed...]
    pallas_call x4 -> x3, Pallas kernels: 95.2 us -> 34.8 us  [call(): pl.pallas_call(inner, input_output_aliases={start + i: first_out + i for...]
    all_gather x1 -> x0, waiting for transfers between devices: 31.1 us -> none  [fast_body(): everyone = lax.all_gather(vectors, ('dp', 'seq'), axis=0)]
    ppermute x2 -> x0, waiting for transfers between devices: 15.3 us -> none  [the longest x1 15.3 us: fast_body(): got_time = lax.ppermute(own_time, 'seq', swap)]
    pallas_call x1, Pallas kernels: 113 us -> 101 us  [fast_body(): pl.pallas_call(back_kernel, grid=(pairs + 2,), in_specs=[near(0), near(pa...]
    unnamed x46 -> x22, local copies, waits for them, and re-layouts: 7.63 us -> 0.95 us
    reduce_sum x3 -> x0, other arithmetic: 4.62 us -> none  [the longest x2 3 us: fast_body(): jnp.sum(shard_of(a, w), 0)]
  transfers between devices with their start and end apart: 5 -> 2, of which waited for: 3 -> 1; matrix products, arithmetic and copies ran while one was open for 3% -> 2% of each run, Pallas kernels for 12% -> 16%
where the time goes in v1:
time: 224 us; the launch traced here: 223 us
  Pallas kernels  204 us (91%)
  local copies, waits for them, and re-layouts  5.87 us (3%)
  waiting for transfers between devices  5.55 us (2%)
  starting transfers between devices  3.21 us (1%)
  other arithmetic  2.7 us (1%)
    pallas_call x1, Pallas kernels, fast_body(): pl.pallas_call(back_kernel, grid=(pairs + 2,), in_specs=[near(0), near(pa...  101 us
    pallas_call x1, Pallas kernels, fast_body(): pl.pallas_call(middle_kernel, grid=(tiles,), in_specs=[own_part] + [fixed...  64.6 us
    pallas_call x3, Pallas kernels, call(): pl.pallas_call(inner, input_output_aliases={start + i: first_out + i for...  34.8 us
    ppermute x1, waiting for transfers between devices, fast_body(): other = lax.ppermute(theirs(tokens), 'seq', swap)  5.55 us
  transfers between devices with their start and end apart: 2, of which 1 were waited for; matrix products, arithmetic and copies ran while one was open for 2% of the time, Pallas kernels for 16%

profile of v1, /device:TPU:0, one launch (start us, length us, event | category | flops | bytes accessed | tf_op | source)
XLA Modules:
  0.0 222.9 jit_solution(12685347173195635681)
XLA Ops:
  0.6 0.0 copy-start.5
  0.7 0.0 copy-start.10
  0.7 0.0 copy-start
  0.7 1.3 dynamic-slice_bitcast_fusion.2
  2.0 3.0 %collective-permute-start = (bf16[512,768]{1,0:T(8,128)(2,1)S(1)}, bf16[512,768]{1,0:T(8,128)(2,1)S(1)}, u32[]{:S(2)}, u32[]{:S(2)}) collective-permute-start(bf16[512,768]{1,0:T(8,128)(2,1)S(1)} %dynamic-slice_bitcast_fusion.2), channel_id=1, source_target_pairs={{0,1},{1,0},{2,3},{3,2},{4,5},{5,4},{6,7},{7,6},{8,9},{9,8},{10,11... | collective-permute-start | bytes 2359304 | tf_op jit(solution)/shard_map/ppermute | solution.py:1329
  5.0 0.0 copy-done.5
  5.0 0.0 copy-done.10
  5.0 0.1 compare_and_fusion
  5.1 0.0 copy-done
  5.1 0.2 broadcast_select_fusion
  5.3 0.0 copy-start.6
  5.3 0.0 copy-start.7
  5.3 0.0 copy-start.8
  5.4 0.0 copy-start.4
  5.4 0.0 copy-start.1
  5.4 0.0 copy-start.9
  5.4 0.0 copy-start.3
  5.4 1.3 dynamic-slice_bitcast_fusion
  6.7 0.2 collective-permute-start.1
  6.8 0.0 copy-done.6
  6.8 0.6 reshape.40.refs_3_.gain_ref
  7.4 0.0 copy-done.7
  7.4 0.6 reshape.41.gain_ref
  8.0 0.0 copy-done.8
  8.0 0.6 reshape.43.down_bias_ref
  8.6 0.0 copy-done.4
  8.6 0.6 broadcast_in_dim.46
  9.2 0.0 copy-done.1
  9.2 0.0 copy-done.9
  9.2 0.4 convolution_reduce_fusion
  9.6 0.0 copy-done.3
  9.7 0.6 reshape.38.refs_2_.mod_ref
  10.3 0.6 pad_add_fusion.refs_0_
  10.9 7.0 %project.2 = (bf16[768,1024]{1,0:T(8,128)(2,1)}, bf16[1024,2304]{1,0:T(8,128)(2,1)}) custom-call(s32[2]{0:T(128)} %pad_add_fusion.refs_0_, bf16[2,512,768]{2,1,0:T(8,128)(2,1)} %own_hbm.1, f32[6,768]{1,0:T(8,128)} %reshape.38.refs_2_.mod_ref, f32[1,768]{1,0:T(1,128)} %reshape.40.refs_3_.gain_ref, bf16[768,2304]{1,0:T(8,128)(2,1)} %weight_hbm.1, ...), custom_call_target="tpu_custom_call" | custom-call | flops 1811939328 | bytes 6291456 | tf_op jit(solution)/shard_map/project/pallas_call | solution.py:1273
  17.8 5.5 %collective-permute-done.refs_1_.other_ref.other_hbm = bf16[512,768]{1,0:T(8,128)(2,1)S(1)} collective-permute-done((bf16[512,768]{1,0:T(8,128)(2,1)S(1)}, bf16[512,768]{1,0:T(8,128)(2,1)S(1)}, u32[]{:S(2)}, u32[]{:S(2)}) %collective-permute-start) | collective-permute-done | bytes 786464 | tf_op jit(solution)/shard_map/ppermute | solution.py:1329
  23.4 0.0 copy-start.2
  23.4 0.9 copy-done.2
  24.3 7.0 %project.3 = (bf16[768,1024]{1,0:T(8,128)(2,1)}, bf16[1024,2304]{1,0:T(8,128)(2,1)}) custom-call(s32[2]{0:T(128)} %pad_add_fusion.refs_0_, bf16[512,768]{1,0:T(8,128)(2,1)} %copy-done.2, f32[6,768]{1,0:T(8,128)} %reshape.38.refs_2_.mod_ref, f32[1,768]{1,0:T(1,128)} %reshape.40.refs_3_.gain_ref, ...), custom_call_target="tpu_custom_call", output_to_operand_aliasing={{0}: (7, {}), {1}: (8, {})} | custom-call | flops 1811939328 | bytes 6291456 | tf_op jit(solution)/shard_map/project/pallas_call | solution.py:1273
  31.3 20.8 %attend.1 = (bf16[1024,768]{1,0:T(8,128)(2,1)}, bf16[12,1024,1024]{2,1,0:T(8,128)(2,1)}, f32[1024,768]{1,0:T(8,128)}) custom-call(s32[2]{0:T(128)} %pad_add_fusion.refs_0_, bf16[1024,2304]{1,0:T(8,128)(2,1)} %get-tuple-element.60.refs_1_.refs_2_.refs_3_.q_ref.k_ref.v_ref, bf16[1024,2304]{1,0:T(8,128)(2,1)} %get-tuple-element.60.refs_1_.refs_2_.refs_3_.q_ref.k_ref.v_ref, ...), custom_call_target="tpu_custom_call" | custom-call | flops 12884901888 | bytes 33554432 | tf_op jit(solution)/shard_map/attend/pallas_call | solution.py:1273
  52.1 0.0 collective-permute-done.1.other_cot_ref
  52.1 64.6 %middle.1 = (bf16[2,512,768]{2,1,0:T(8,128)(2,1)}, bf16[512,768]{1,0:T(8,128)(2,1)}, f32[1024,768]{1,0:T(8,128)}, bf16[1024,768]{1,0:T(8,128)(2,1)}, f32[6,768]{...) custom-call(bf16[2,512,768]{2,1,0:T(8,128)(2,1)} %own_hbm.1, ...), custom_call_target="tpu_custom_call" | custom-call | flops 32614907904 | bytes 37748736 | tf_op jit(solution)/shard_map/middle/pallas_call | solution.py:1415
  116.7 100.5 %back.1 = (bf16[2,512,768]{2,1,0:T(8,128)(2,1)}, f32[2,128]{1,0:T(2,128)}, f32[288,128]{1,0:T(8,128)}, f32[1,288]{1,0:T(1,128)}, f32[1,48]{1,0:T(1,128)}, /*inde...) custom-call(bf16[1024,2304]{1,0:T(8,128)(2,1)} %get-tuple-element.60, ...), custom_call_target="tpu_custom_call", output_to_operand_aliasing={{12}: (27, {})} | custom-call | flops 32212254720 | bytes 62914560 | tf_op jit(solution)/shard_map/back/pallas_call | solution.py:1523
  217.2 4.2 %close.1 = (bf16[2,512,768]{2,1,0:T(8,128)(2,1)}, f32[2,128]{1,0:T(2,128)}, f32[288,128]{1,0:T(8,128)}, f32[1,288]{1,0:T(1,128)}, f32[1,48]{1,0:T(1,128)}, /*ind...) custom-call(bf16[2,512,768]{2,1,0:T(8,128)(2,1)} %get-tuple-element., ...), custom_call_target="tpu_custom_call" | custom-call | tf_op jit(solution)/shard_map/close/pallas_call | solution.py:1621
  221.5 1.2 reduce.1
  (2 shorter events, 0.0 us)
Async XLA Ops:
  0.6 4.4 %copy-start.5 = (s32[2,512]{1,0:T(2,128)S(1)}, s32[2,512]{1,0:T(2,128)}, u32[]{:S(2)}) copy-start(s32[2,512]{1,0:T(2,128)} %param.20) | copy-start | bytes 12292
  0.7 4.4 %copy-start.10 = (s32[2]{0:T(128)S(1)}, s32[2]{0:T(128)}, u32[]{:S(2)}) copy-start(s32[2]{0:T(128)} %param.19) | copy-start | bytes 28
  0.7 4.4 %copy-start = (bf16[2,512,768]{2,1,0:T(8,128)(2,1)S(1)}, bf16[2,512,768]{2,1,0:T(8,128)(2,1)}, u32[]{:S(2)}) copy-start(bf16[2,512,768]{2,1,0:T(8,128)(2,1)} %param.21) | copy-start | bytes 4718596
  2.0 21.4 %collective-permute-start = (bf16[512,768]{1,0:T(8,128)(2,1)S(1)}, bf16[512,768]{1,0:T(8,128)(2,1)S(1)}, u32[]{:S(2)}, u32[]{:S(2)}) collective-permute-start(bf16[512,768]{1,0:T(8,128)(2,1)S(1)} %dynamic-slice_bitcast_fusion.2), channel_id=1, source_target_pairs={{0,1},{1,0},{2,3},{3,2},{4,5},{5,4},{6,7},{7,6},{8,9},{9,8},{10,11... | collective-permute-start | bytes 2359304 | tf_op jit(solution)/shard_map/ppermute | solution.py:1329
  5.3 1.5 copy-start.6
  5.3 2.1 copy-start.7
  5.3 2.7 %copy-start.8 = (bf16[768]{0:T(1024)(128)(2,1)S(1)}, bf16[768]{0:T(1024)(128)(2,1)}, u32[]{:S(2)}) copy-start(bf16[768]{0:T(1024)(128)(2,1)} %param.31) | copy-start | bytes 4612
  5.4 3.2 %copy-start.4 = (bf16[3072]{0:T(1024)(128)(2,1)S(1)}, bf16[3072]{0:T(1024)(128)(2,1)}, u32[]{:S(2)}) copy-start(bf16[3072]{0:T(1024)(128)(2,1)} %param.29) | copy-start | bytes 18436
  5.4 3.8 %copy-start.1 = (bf16[4608,128]{1,0:T(8,128)(2,1)S(1)}, bf16[4608,128]{1,0:T(8,128)(2,1)}, u32[]{:S(2)}) copy-start(bf16[4608,128]{1,0:T(8,128)(2,1)} %mod_weight_hbm.1) | copy-start | bytes 3538948
  5.4 3.8 %copy-start.9 = (bf16[2,128]{1,0:T(2,128)(2,1)S(1)}, bf16[2,128]{1,0:T(2,128)(2,1)}, u32[]{:S(2)}) copy-start(bf16[2,128]{1,0:T(2,128)(2,1)} %time_ref.1) | copy-start | bytes 1540
  5.4 4.2 %copy-start.3 = (bf16[4608]{0:T(1024)(128)(2,1)S(1)}, bf16[4608]{0:T(1024)(128)(2,1)}, u32[]{:S(2)}) copy-start(bf16[4608]{0:T(1024)(128)(2,1)} %param.23) | copy-start | bytes 27652
  6.7 45.4 %collective-permute-start.1 = (bf16[512,768]{1,0:T(8,128)(2,1)}, bf16[512,768]{1,0:T(8,128)(2,1)}, u32[]{:S(2)}, u32[]{:S(2)}) collective-permute-start(bf16[512,768]{1,0:T(8,128)(2,1)} %get-tuple-element.103), channel_id=1, source_target_pairs={{0,1},{1,0},{2,3},{3,2},{4,5},{5,4},{6,7},{7,6},{8,9},{9,8},{10,11... | collective-permute-start | bytes 2359304 | tf_op jit(solution)/shard_map/ppermute | solution.py:1334
  23.4 0.9 copy-start.2

commit v2 on v1

--- a/solution.py
+++ b/solution.py
@@ -323,8 +323,7 @@
 
 
 T_ROWS = 256
-MIDDLE_ROWS = 512
-PROJECT_ROWS = 512
+MIDDLE_ROWS = 256
 MIB = 1 << 20
 
 
@@ -348,28 +347,47 @@
     return jnp.where(lane % 64 < 32, left, right)
 
 
-def project_kernel(source_ref, mod_ref, gain_ref, weight_ref, cos_ref, sin_ref, first_t_ref, qkv_ref):
-    rows, model = source_ref.shape
-    lane = lax.broadcasted_iota(jnp.int32, (rows, 128), 1)
-    scaling = gain_ref[...] * (1.0 + mod_ref[1:2])
-    normed, _ = norm_rows(source_ref[...].astype(jnp.float32))
-    first = (normed * scaling + mod_ref[0:1]).astype(jnp.bfloat16)
-    first_t_ref[...] = first.T
-    for part in range(3):
-        projected = dot(first, weight_ref[:, part * model : (part + 1) * model], 1, 0)
-        for block in range(model // 128):
-            piece = projected[:, block * 128 : (block + 1) * 128]
-            if part < 2:
-                piece = piece * cos_ref[...] + swap_halves(piece, lane) * sin_ref[...]
-            piece = piece.astype(jnp.bfloat16)
-            if part == 0:
-                piece = piece * 0.125
-            column = part * model + block * 128
-            qkv_ref[:, column : column + 128] = piece
-
-
-def attend_kernel(q_ref, k_ref, v_ref, out_ref, exp_ref, inv_ref):
+def attend_kernel(
+    prefix_ref,
+    q_ref,
+    k_ref,
+    v_ref,
+    mask_ref,
+    cot_hbm,
+    out_ref,
+    exp_ref,
+    inv_ref,
+    own_live_ref,
+    other_live_ref,
+    other_cot_hbm,
+    give,
+    got,
+    sems,
+):
     rows = 128
+    step = pl.program_id(0)
+    links = Links()
+    half = mask_ref.shape[1]
+    partner = links.partner["Y"]
+
+    def exchanges():
+        return [
+            remote(give, got, sems, 0, partner),
+            remote(cot_hbm.at[1 - links.me], other_cot_hbm, sems, 1, partner),
+        ]
+
+    @pl.when(step == 0)
+    def _():
+        position = links.me * half + lax.broadcasted_iota(jnp.int32, (1, half), 1)
+        live = [
+            jnp.where((position >= prefix_ref[i]) & (mask_ref[i : i + 1] == 1), 1.0, 0.0) for i in range(2)
+        ]
+        wide = [jnp.broadcast_to(row, (8, half)) for row in live]
+        own_live_ref[...] = jnp.where(links.me == 0, wide[0], wide[1])
+        give[...] = jnp.where(links.me == 0, wide[1], wide[0])
+        links.greet(("Y",))
+        start_all(exchanges())
+
     length = q_ref.shape[0]
     lane = lax.broadcasted_iota(jnp.int32, (rows, 128), 1)
     keys = k_ref[...]
@@ -392,6 +410,12 @@
         out_ref[at] = jnp.where(lane < 64, outs[0], outs[1]).astype(jnp.bfloat16)
         inv_ref[at] = jnp.where(lane < 64, inverses[0], inverses[1])
 
+    @pl.when(step == pl.num_programs(0) - 1)
+    def _():
+        for copy in exchanges():
+            copy.wait()
+        other_live_ref[...] = got[...]
+
 
 def share(core, grad, keep_ref, send_ref, *at):
     first, second = grad
@@ -404,6 +428,8 @@
     other_ref,
     own_cot_ref,
     other_cot_ref,
+    own_live_ref,
+    other_live_ref,
     attended_ref,
     mod_ref,
     gain_ref,
@@ -550,6 +576,11 @@
         at = chunk * rows
         return (first_ref if at < half else second_ref)[at % half : at % half + rows]
 
+    def live_cot(chunk):
+        at = (chunk * rows) % half
+        live = (own_live_ref if chunk * rows < half else other_live_ref)[...].T[at : at + rows, 0:1]
+        return pick(own_cot_ref, other_cot_ref, chunk).astype(jnp.float32) * live
+
     @pl.when(step == 0)
     def _():
         bias_grad = jnp.zeros((1, model), jnp.float32)
@@ -565,7 +596,7 @@
             place = (chunk * rows) % half
             (own_out_ref if chunk * rows < half else other_out_ref)[place : place + rows] = rounded
             second_t[:, at] = rounded.T
-            grad = (gate_two * pick(own_cot_ref, other_cot_ref, chunk).astype(jnp.float32)).astype(jnp.bfloat16)
+            grad = (gate_two * live_cot(chunk)).astype(jnp.bfloat16)
             grad_two[at] = grad
             bias_grad = bias_grad + jnp.sum(grad.astype(jnp.float32), 0, keepdims=True)
         rows_ref[5:6] = bias_grad
@@ -619,7 +650,7 @@
             output = (middle + gate_two * branch_two).astype(jnp.bfloat16)
             place = (chunk * rows) % half
             (own_out_ref if chunk * rows < half else other_out_ref)[place : place + rows] = output
-            cot = pick(own_cot_ref, other_cot_ref, chunk).astype(jnp.float32)
+            cot = live_cot(chunk)
             grad = sum_second[at]
             weighted = grad * normed
             scaled = grad * scaling
@@ -668,11 +699,12 @@
     def place(self):
         return self.me * 16 + self.bit["X"] * 8 + self.bit["W"] * 4 + self.bit["Z"] * 2 + self.bit["C"]
 
-    def greet(self):
+    def greet(self, names=("C", "X", "Z", "W", "ZW", "Y")):
         barrier = pltpu.get_barrier_semaphore()
-        for device in self.partner.values():
+        for name in names:
+            device = self.partner[name]
             pl.semaphore_signal(barrier, inc=1, device_id=device, device_id_type=pl.DeviceIdType.MESH)
-        pl.semaphore_wait(barrier, len(self.partner))
+        pl.semaphore_wait(barrier, len(names))
 
 
 def flips_of(kind):
@@ -815,7 +847,7 @@
 
 BACK_COPIES = sum(copies_of(spec) for spec in BACK_PIECES)
 HOPS = (("C",), Z_FLIPS, ("X",), ("Y",))
-SPREAD = "XZWCY"
+RUNNING = "CXZWY"
 
 
 def spread_copies(links, array, sems, slot, number):
@@ -834,6 +866,103 @@
 def receive_all(copies):
     for copy in copies:
         copy.wait_recv()
+
+
+def front_kernel(
+    tokens_hbm,
+    time_ref,
+    mod_weight_hbm,
+    mod_bias_ref,
+    gain_ref,
+    weight_hbm,
+    cos_hbm,
+    sin_hbm,
+    first_t_ref,
+    qkv_hbm,
+    other_hbm,
+    mod_ref,
+    other_ref,
+    own,
+    mod_weight,
+    weight,
+    cos_ref,
+    sin_ref,
+    qkv,
+    sems,
+    local_sems,
+    store_sems,
+):
+    rows = T_ROWS
+    half, model = own.shape
+    blocks = half // rows
+    links = Links()
+
+    def exchange(block):
+        at = pl.ds(block * rows, rows)
+        return remote(tokens_hbm.at[1 - links.me, at], other_ref.at[at], sems, block, links.partner["Y"])
+
+    def fetches():
+        pairs = (
+            (mod_weight_hbm, mod_weight),
+            (tokens_hbm.at[links.me], own),
+            (weight_hbm, weight),
+            (cos_hbm.at[links.me], cos_ref),
+            (sin_hbm.at[links.me], sin_ref),
+        )
+        return [pltpu.make_async_copy(a, b, local_sems.at[i]) for i, (a, b) in enumerate(pairs)]
+
+    def store(block):
+        at = pl.ds(block * rows, rows)
+        return pltpu.make_async_copy(qkv.at[at], qkv_hbm.at[at], store_sems.at[block])
+
+    def store_other(block):
+        at = pl.ds(block * rows, rows)
+        return pltpu.make_async_copy(other_ref.at[at], other_hbm.at[at], store_sems.at[2 * blocks + block])
+
+    for copy in fetches():
+        copy.start()
+    links.greet(("Y",))
+    for block in range(blocks):
+        exchange(block).start()
+    for copy in fetches():
+        copy.wait()
+    embedding = time_ref[...].astype(jnp.float32)
+    embedding = jnp.where(links.me == 0, embedding[0:1], embedding[1:2])
+    embedding = jnp.broadcast_to(embedding, (16, embedding.shape[1])).astype(jnp.bfloat16)
+    modulation = dot(embedding, mod_weight[...], 1, 1)[0:1] + mod_bias_ref[...].astype(jnp.float32)
+    parts = [modulation[:, i * model : (i + 1) * model] for i in range(6)]
+    for i in range(6):
+        mod_ref[i : i + 1] = parts[i]
+    lane = lax.broadcasted_iota(jnp.int32, (rows, 128), 1)
+    scaling = gain_ref[...].astype(jnp.float32) * (1.0 + parts[1])
+    for block in range(2 * blocks):
+        if block < blocks:
+            source = own[block * rows : (block + 1) * rows]
+        else:
+            exchange(block - blocks).wait_recv()
+            source = other_ref[(block - blocks) * rows : (block - blocks + 1) * rows]
+            store_other(block - blocks).start()
+        at = slice(block * rows, (block + 1) * rows)
+        normed, _ = norm_rows(source.astype(jnp.float32))
+        first = (normed * scaling + parts[0]).astype(jnp.bfloat16)
+        first_t_ref[:, at] = first.T
+        for part in range(3):
+            projected = dot(first, weight[:, part * model : (part + 1) * model], 1, 0)
+            for column in range(model // 128):
+                piece = projected[:, column * 128 : (column + 1) * 128]
+                if part < 2:
+                    piece = piece * cos_ref[at] + swap_halves(piece, lane) * sin_ref[at]
+                piece = piece.astype(jnp.bfloat16)
+                if part == 0:
+                    piece = piece * 0.125
+                start = part * model + column * 128
+                qkv[at, start : start + 128] = piece
+        store(block).start()
+    for block in range(2 * blocks):
+        store(block).wait()
+    for block in range(blocks):
+        store_other(block).wait()
+        exchange(block).wait_send()
 
 
 def back_kernel(
@@ -946,7 +1075,7 @@
     tail_slot = running_slot + 5
 
     def running_copy(number):
-        partner = links.partner[SPREAD[number]]
+        partner = links.partner[RUNNING[number]]
         return remote(running.at[number], running_got.at[number], sems, running_slot + number, partner)
 
     def tail_copy():
@@ -977,19 +1106,21 @@
         start_all(spread_copies(links, early, sems, early_slot, 0))
         running_copy(0).start()
 
-    for number in range(1, 6):
-
-        @pl.when(step == number)
+    for number in range(4):
+
+        @pl.when(step == number + 1)
         def _(number=number):
-            if number < 5:
-                receive_all(spread_copies(links, early, sems, early_slot, number - 1))
-                if number < 4:
-                    start_all(spread_copies(links, early, sems, early_slot, number))
-            running_copy(number - 1).wait_recv()
-            running[number] = running[number - 1] + running_got[number - 1]
-            if number < 5:
-                running_copy(number).start()
-                block_copy(number - 1).start()
+            block_copy(number).start()
+
+    def early_arrive(number):
+        receive_all(spread_copies(links, early, sems, early_slot, number))
+
+    def early_start(number):
+        start_all(spread_copies(links, early, sems, early_slot, number))
+
+    def running_arrive(number):
+        running_copy(number).wait_recv()
+        running[number + 1] = running[number] + running_got[number]
 
     def at_step(number):
         return pl.when(step == number)
@@ -1000,12 +1131,20 @@
             for copy in fetches(0, 5):
                 copy.wait()
             down_tail_give[...] = down_tail[1 - links.bit["X"]]
+            early_arrive(0)
+            running_arrive(0)
+            early_start(1)
+            running_copy(1).start()
             tail_copy().start()
             upv.step()
             upx.step()
 
         @at_step(1)
         def _():
+            early_arrive(1)
+            running_arrive(1)
+            early_start(2)
+            running_copy(2).start()
             tail_copy().wait_recv()
             kept = down_tail[links.bit["X"]].astype(jnp.float32) + down_tail_got[...].astype(jnp.float32)
             down.keep[3] = kept.astype(jnp.bfloat16)
@@ -1021,6 +1160,10 @@
 
         @at_step(3)
         def _():
+            early_arrive(2)
+            running_arrive(2)
+            early_start(3)
+            running_copy(3).start()
             ins[0].step()
 
         @at_step(4)
@@ -1030,6 +1173,8 @@
 
         @at_step(5)
         def _():
+            running_arrive(3)
+            running_copy(4).start()
             ins[1].step()
             ins[0].step()
 
@@ -1189,6 +1334,8 @@
             if number < 3:
                 start_all(spread_copies(links, late, sems, late_slot, number + 1))
 
+        early_arrive(3)
+        running_arrive(4)
         ins[0].last()
         hop_on()
         ins[1].last()
@@ -1257,38 +1404,6 @@
     sines = np.concatenate([-sines, sines, -sines, sines], 1)
     both = [np.stack([t, np.roll(t, -(length // 2), 0)]).astype(np.float32) for t in (cosine, sines)]
     return jnp.asarray(both[0]), jnp.asarray(both[1])
-
-
-def call(kernel, grid, place, in_specs, out_specs, out_shape, scratch, operands, name, flops, moved, after=(), alias=()):
-    count = len(in_specs) + 1
-    extra = len(after) + len(alias)
-    in_specs = in_specs + [pl.BlockSpec(memory_space=pl.ANY)] * extra
-
-    def inner(*refs):
-        kernel(*refs[:count], *refs[count + extra :])
-
-    start = count + len(after)
-    first_out = len(out_shape) - len(alias)
-    operands = (*operands, *after, *alias)
-    return pl.pallas_call(
-        inner,
-        input_output_aliases={start + i: first_out + i for i in range(len(alias))},
-        grid_spec=pltpu.PrefetchScalarGridSpec(
-            num_scalar_prefetch=1, grid=grid, in_specs=in_specs, out_specs=out_specs, scratch_shapes=scratch
-        ),
-        out_shape=out_shape,
-        compiler_params=params(),
-        cost_estimate=pl.CostEstimate(flops=flops, bytes_accessed=moved, transcendentals=0),
-        name=name,
-    )(place, *operands)
-
-
-def whole(*shape):
-    return pl.BlockSpec(shape, lambda i, p: (0,) * len(shape))
-
-
-def swap_pairs(size, bit):
-    return [(i, i ^ bit) for i in range(size)]
 
 
 def fast_body(
@@ -1314,87 +1429,99 @@
     length = 2 * half
     hidden_width = feed_up.shape[1]
     size = lax.axis_size("dp")
-    me = lax.axis_index("seq")
-    dp = lax.axis_index("dp")
-    place = jnp.stack([dp % 2, me]).astype(jnp.int32)
-    swap = swap_pairs(2, 1)
     shape = jax.ShapeDtypeStruct
 
-    def mine(array):
-        return lax.dynamic_index_in_dim(array, me, 0, False)
-
-    def theirs(array):
-        return lax.dynamic_index_in_dim(array, 1 - me, 0, False)
-
-    other = lax.ppermute(theirs(tokens), "seq", swap)
-    positions = me * half + jnp.arange(half, dtype=jnp.int32)
-    live = (positions[None, :] >= prefix_length[:, None]) & (suffix_mask == 1)
-    live_cot = jnp.where(live[:, :, None], cotangent, jnp.zeros_like(cotangent))
-    own_cot = mine(live_cot)
-    other_cot = lax.ppermute(theirs(live_cot), "seq", swap)
-
-    modulation = jnp.einsum(
-        "c,oc->o", mine(time_embedding), modulation_weight, preferred_element_type=f32
-    ) + modulation_bias.astype(f32)
-    modulation = modulation.reshape(6, model)
-    gain_one = attention_gain.astype(f32)[None]
-    gain_two = feed_gain.astype(f32)[None]
+    packed = [modulation_bias, attention_gain, feed_gain, feed_down_bias, feed_up_bias]
+    packed = jnp.concatenate(packed).astype(f32)[None]
+
+    def packed_at(number):
+        return pl.BlockSpec((1, model), lambda h: (0, number), pipeline_mode=pl.Buffered(1))
+
     cosine, sines = turn_tables(length)
-    table = pl.BlockSpec((None, length, 128), lambda i, p: (p[1], 0, 0))
-    own_rows = pl.BlockSpec((None, half, model), lambda i, p: (p[1], 0, 0))
-    blocks = half // PROJECT_ROWS
-
-    def project(source, spec, start, alias):
-        turn = pl.BlockSpec((None, PROJECT_ROWS, 128), lambda i, p: (p[1], i + start, 0))
-        return call(
-            lambda p, *refs: project_kernel(*refs),
-            (blocks,),
-            place,
-            [spec, whole(6, model), whole(1, model), whole(model, 3 * model), turn, turn],
-            [
-                pl.BlockSpec((model, PROJECT_ROWS), lambda i, p: (0, i + start)),
-                pl.BlockSpec((PROJECT_ROWS, 3 * model), lambda i, p: (i + start, 0)),
-            ],
-            [shape((model, length), bf16), shape((length, 3 * model), bf16)],
-            [],
-            (source, modulation, gain_one, attention_in, cosine, sines),
-            "project",
-            length * model * 3 * model,
-            6 * MIB,
-            alias=alias,
-        )
-
-    kept = project(tokens, pl.BlockSpec((None, PROJECT_ROWS, model), lambda i, p: (p[1], i, 0)), 0, ())
-    first_t, qkv = project(other, pl.BlockSpec((PROJECT_ROWS, model), lambda i, p: (i, 0)), blocks, kept)
+    anywhere = pl.BlockSpec(memory_space=pl.ANY)
+
+    def fixed(*dims):
+        return pl.BlockSpec(dims, lambda h: (0,) * len(dims), pipeline_mode=pl.Buffered(1))
+
+    first_t, qkv, other, modulation = pl.pallas_call(
+        front_kernel,
+        grid=(1,),
+        in_specs=[
+            anywhere,
+            fixed(2, 128),
+            anywhere,
+            fixed(1, 6 * model),
+            packed_at(6),
+            anywhere,
+            anywhere,
+            anywhere,
+        ],
+        out_specs=[fixed(model, length), anywhere, anywhere, fixed(6, model)],
+        out_shape=[
+            shape((model, length), bf16),
+            shape((length, 3 * model), bf16),
+            shape((half, model), bf16),
+            shape((6, model), f32),
+        ],
+        scratch_shapes=[
+            pltpu.VMEM((half, model), bf16),
+            pltpu.VMEM((half, model), bf16),
+            pltpu.VMEM((6 * model, 128), bf16),
+            pltpu.VMEM((model, 3 * model), bf16),
+            pltpu.VMEM((length, 128), f32),
+            pltpu.VMEM((length, 128), f32),
+            pltpu.VMEM((length, 3 * model), bf16),
+            pltpu.SemaphoreType.DMA((2, half // T_ROWS)),
+            pltpu.SemaphoreType.DMA((5,)),
+            pltpu.SemaphoreType.DMA((3 * half // T_ROWS,)),
+        ],
+        compiler_params=pltpu.CompilerParams(vmem_limit_bytes=62 * MIB, collective_id=2, has_side_effects=True),
+        cost_estimate=pl.CostEstimate(flops=2 * length * model * 3 * model, bytes_accessed=16 * MIB, transcendentals=0),
+        name="front",
+    )(tokens, time_embedding, modulation_weight, packed, packed, attention_in, cosine, sines)
+
     def column(k):
-        return pl.BlockSpec((length, 128), lambda h, p: (0, h + k))
+        return pl.BlockSpec((length, 128), lambda h: (0, h + k))
 
     pairs = model // 128
-    exps_block = pl.BlockSpec((2, length, length), lambda h, p: (h, 0, 0))
-    attended, exps, inverses = call(
-        lambda p, *refs: attend_kernel(*refs),
-        (pairs,),
-        place,
-        [column(0), column(pairs), column(2 * pairs)],
-        [column(0), exps_block, column(0)],
-        [shape((length, model), bf16), shape((HEADS, length, length), bf16), shape((length, model), f32)],
-        [],
-        (qkv, qkv, qkv),
-        "attend",
-        16 * length * length * model,
-        32 * MIB,
-    )
+    attended, exps, inverses, own_live, other_live, other_cot = pl.pallas_call(
+        attend_kernel,
+        grid=(pairs,),
+        in_specs=[
+            pl.BlockSpec(memory_space=pltpu.SMEM),
+            column(0),
+            column(pairs),
+            column(2 * pairs),
+            fixed(2, half),
+            anywhere,
+        ],
+        out_specs=[
+            column(0),
+            pl.BlockSpec((2, length, length), lambda h: (h, 0, 0)),
+            column(0),
+            fixed(8, half),
+            fixed(8, half),
+            anywhere,
+        ],
+        out_shape=[
+            shape((length, model), bf16),
+            shape((HEADS, length, length), bf16),
+            shape((length, model), f32),
+            shape((8, half), f32),
+            shape((8, half), f32),
+            shape((half, model), bf16),
+        ],
+        scratch_shapes=[pltpu.VMEM((8, half), f32), pltpu.VMEM((8, half), f32), pltpu.SemaphoreType.DMA((2, 2))],
+        compiler_params=pltpu.CompilerParams(vmem_limit_bytes=60 * MIB, collective_id=3, has_side_effects=True),
+        cost_estimate=pl.CostEstimate(flops=16 * length * length * model, bytes_accessed=32 * MIB, transcendentals=0),
+        name="attend",
+    )(prefix_length, qkv, qkv, qkv, suffix_mask, cotangent)
 
     tiles = 4
     width = hidden_width // tiles
     groups = size // 2
     share_rows = hidden_width // size
     model_rows = model // size
-    anywhere = pl.BlockSpec(memory_space=pl.ANY)
-
-    def fixed(*dims):
-        return pl.BlockSpec(dims, lambda h: (0,) * len(dims), pipeline_mode=pl.Buffered(1))
-
     own_part = pl.BlockSpec((None, half, model), lambda h: (lax.axis_index("seq"), 0, 0), pipeline_mode=pl.Buffered(1))
     up_tile = pl.BlockSpec((model, width), lambda j: (0, j))
     bias_tile = pl.BlockSpec((1, width), lambda j: (0, j))
@@ -1415,17 +1542,16 @@
     ) = pl.pallas_call(
         middle_kernel,
         grid=(tiles,),
-        in_specs=[own_part]
-        + [fixed(half, model)] * 3
+        in_specs=[own_part, fixed(half, model), own_part, fixed(half, model), fixed(8, half), fixed(8, half)]
         + [
             fixed(length, model),
             fixed(6, model),
-            fixed(1, model),
+            packed_at(7),
             fixed(model, model),
             up_tile,
-            bias_tile,
+            pl.BlockSpec((1, width), lambda j: (0, j + 9)),
             down_tile,
-            fixed(1, model),
+            packed_at(8),
         ],
         out_specs=[
             own_part,
@@ -1468,16 +1594,18 @@
     )(
         tokens,
         other,
-        own_cot,
+        cotangent,
         other_cot,
+        own_live,
+        other_live,
         attended,
         modulation,
-        gain_two,
+        packed,
         attention_out,
         feed_up,
-        feed_up_bias.astype(f32)[None],
+        packed,
         feed_down,
-        feed_down_bias.astype(f32)[None],
+        packed,
     )
     merge = (2, (tiles - 1) * model_rows, model)
 
@@ -1535,7 +1663,7 @@
             turn,
             *[anywhere] * 5,
             fixed(6, model),
-            fixed(1, model),
+            packed_at(6),
         ]
         + [anywhere] * 6
         + [fixed(6, model), fixed(1, hidden_width), fixed(2, 128), anywhere, anywhere, anywhere],
@@ -1590,7 +1718,7 @@
         other,
         grad_middle,
         modulation,
-        gain_one,
+        packed,
         down_sum,
         down_tail,
         upv_sum.reshape(merge),
@@ -1648,7 +1776,7 @@
     sequences, half, model = tokens.shape
     size = lax.axis_size("dp")
     fits = model % (16 * size) == 0 and half % T_ROWS == 0
-    fits = fits and tokens.shape[1] % PROJECT_ROWS == 0 and rest[10].shape[1] == 4 * model and size == 16 and lax.axis_size("seq") == 2 and sequences == 2
+    fits = fits and tokens.shape[1] % MIDDLE_ROWS == 0 and rest[10].shape[1] == 4 * model and size == 16 and lax.axis_size("seq") == 2 and sequences == 2
     return (fast_body if fits else general_body)(tokens, *rest)
 
 

time: 224 us -> 217 us (0.969)
  Pallas kernels: 204 us -> 210 us
  waiting for transfers between devices: 5.55 us -> 0 us
  starting transfers between devices: 3.21 us -> 0 us
  local copies, waits for them, and re-layouts: 5.87 us -> 3.5 us
    pallas_call x4 -> x3, Pallas kernels: 99.4 us -> 124 us  [the longest x1 75.9 us: fast_body(): pl.pallas_call(middle_kernel, grid=(tiles,), in_specs=[own_part, fixed(ha...]
    pallas_call x1, Pallas kernels: 101 us -> 81.9 us  [fast_body(): pl.pallas_call(back_kernel, grid=(pairs + 2,), in_specs=[near(0), near(pa...]
    ppermute x2 -> x0, waiting for transfers between devices: 5.55 us -> none  [the longest x1 5.55 us: fast_body(): other = lax.ppermute(theirs(tokens), 'seq', swap)]
    ppermute x2 -> x0, starting transfers between devices: 3.21 us -> none  [the longest x1 3.03 us: fast_body(): other = lax.ppermute(theirs(tokens), 'seq', swap)]
    squeeze x2 -> x0, local copies, waits for them, and re-layouts: 2.56 us -> none  [theirs(): return lax.dynamic_index_in_dim(array, 1 - me, 0, False)]
  transfers between devices with their start and end apart: 2 -> 0, of which waited for: 1 -> 0; matrix products, arithmetic and copies ran while one was open for 2% -> 0% of each run, Pallas kernels for 16% -> 0%
where the time goes in v2:
time: 217 us; the launch traced here: 216 us
  Pallas kernels  210 us (97%)
  local copies, waits for them, and re-layouts  3.5 us (2%)
    pallas_call x1, Pallas kernels, fast_body(): pl.pallas_call(back_kernel, grid=(pairs + 2,), in_specs=[near(0), near(pa...  81.9 us
    pallas_call x1, Pallas kernels, fast_body(): pl.pallas_call(middle_kernel, grid=(tiles,), in_specs=[own_part, fixed(ha...  75.9 us
    pallas_call x1, Pallas kernels, fast_body(): pl.pallas_call(front_kernel, grid=(1,), in_specs=[anywhere, fixed(2, 128)...  25.2 us
    pallas_call x1, Pallas kernels, fast_body(): pl.pallas_call(attend_kernel, grid=(pairs,), in_specs=[pl.BlockSpec(memor...  22.7 us

profile of v2, /device:TPU:0, one launch (start us, length us, event | category | flops | bytes accessed | tf_op | source)
XLA Modules:
  0.0 216.3 jit_solution(17190389501058824682)
XLA Ops:
  0.6 0.7 reshape_dynamic-update-slice_fusion
  1.4 0.7 constant_dynamic-update-slice_fusion.2
  2.1 0.7 constant_dynamic-update-slice_fusion.1
  2.7 0.7 constant_dynamic-update-slice_fusion
  3.4 0.7 reshape_dynamic-update-slice_fusion.1
  4.1 0.7 convert_element_type.10.mod_bias_ref.gain_ref.up_bias_ref.down_bias_ref
  4.8 25.2 %front.1 = (bf16[768,1024]{1,0:T(8,128)(2,1)}, bf16[1024,2304]{1,0:T(8,128)(2,1)}, bf16[512,768]{1,0:T(8,128)(2,1)}, f32[6,768]{1,0:T(8,128)}) custom-call(bf16[2,512,768]{2,1,0:T(8,128)(2,1)} %own_hbm.1, bf16[2,128]{1,0:T(2,128)(2,1)} %time_ref.3, bf16[4608,128]{1,0:T(8,128)(2,1)} %mod_weight_hbm.3, ...), custom_call_target="tpu_custom_call" | custom-call | flops 3623878656 | bytes 16777216 | tf_op jit(solution)/shard_map/front/pallas_call | solution.py:1446
  30.1 22.7 %attend.1 = (bf16[1024,768]{1,0:T(8,128)(2,1)}, bf16[12,1024,1024]{2,1,0:T(8,128)(2,1)}, f32[1024,768]{1,0:T(8,128)}, f32[8,512]{1,0:T(8,128)}, f32[8,512]{1,0:T(8,128)}, /*index=5*/bf16[512,768]{1,0:T(8,128)(2,1)}) custom-call(s32[2]{0:T(128)} %prefix_ref.1, bf16[1024,2304]{1,0:T(8,128)(2,1)} %get-tuple-element.61.q_ref.k_ref.v_ref, ...), custom_call_target="tpu_custom_call" | custom-call | flops 12884901888 | bytes 33554432 | tf_op jit(solution)/shard_map/attend/pallas_call | solution.py:1487
  52.8 75.9 %middle.1 = (bf16[2,512,768]{2,1,0:T(8,128)(2,1)}, bf16[512,768]{1,0:T(8,128)(2,1)}, f32[1024,768]{1,0:T(8,128)}, bf16[1024,768]{1,0:T(8,128)(2,1)}, f32[6,768]{...) custom-call(bf16[2,512,768]{2,1,0:T(8,128)(2,1)} %own_hbm.1, ...), custom_call_target="tpu_custom_call" | custom-call | flops 32614907904 | bytes 37748736 | tf_op jit(solution)/shard_map/middle/pallas_call | solution.py:1542
  128.7 81.9 %back.1 = (bf16[2,512,768]{2,1,0:T(8,128)(2,1)}, f32[2,128]{1,0:T(2,128)}, f32[288,128]{1,0:T(8,128)}, f32[1,288]{1,0:T(1,128)}, f32[1,48]{1,0:T(1,128)}, /*inde...) custom-call(bf16[1024,2304]{1,0:T(8,128)(2,1)} %get-tuple-element.61, ...), custom_call_target="tpu_custom_call", output_to_operand_aliasing={{12}: (27, {})} | custom-call | flops 32212254720 | bytes 62914560 | tf_op jit(solution)/shard_map/back/pallas_call | solution.py:1651
  210.6 4.2 %close.1 = (bf16[2,512,768]{2,1,0:T(8,128)(2,1)}, f32[2,128]{1,0:T(2,128)}, f32[288,128]{1,0:T(8,128)}, f32[1,288]{1,0:T(1,128)}, f32[1,48]{1,0:T(1,128)}, /*ind...) custom-call(bf16[2,512,768]{2,1,0:T(8,128)(2,1)} %get-tuple-element., ...), custom_call_target="tpu_custom_call" | custom-call | tf_op jit(solution)/shard_map/close/pallas_call | solution.py:1749
  214.8 1.3 reduce

commit v3 on v2

--- a/solution.py
+++ b/solution.py
@@ -323,6 +323,7 @@
 
 
 T_ROWS = 256
+FRONT_ROWS = 128
 MIDDLE_ROWS = 256
 MIB = 1 << 20
 
@@ -892,7 +893,7 @@
     local_sems,
     store_sems,
 ):
-    rows = T_ROWS
+    rows = FRONT_ROWS
     half, model = own.shape
     blocks = half // rows
     links = Links()
@@ -1256,45 +1257,28 @@
     def home():
         return pltpu.make_async_copy(tokens_stage.at[pl.ds(0, half)], tokens_grad_ref.at[links.me], local_sems.at[11])
 
-    def vectors():
-        middle = model // 2
-        for m in range(6):
-            source, row = (late, 2 * m) if m < 2 else (early, 2 * m - 4)
-            by_vector[m, :, 0:middle] = source[:, row, :]
-            by_vector[m, :, middle:model] = source[:, row + 1, :]
-        ones = jnp.ones((32, 128), jnp.float32)
-        factors = jnp.concatenate([late[:, 6, 0:128], ones], 1)
-        unit = mod_weight_grad_ref.shape[0] // 6
-        for part in range(6):
-            at = dp * 6 + part
-            product = lax.dot_general(
-                by_vector[at // 16],
-                factors,
-                (((0,), (0,)), ((), ())),
-                precision=highest,
-                preferred_element_type=jnp.float32,
-            )
-            spread[...] = product
-            kept = spread[pl.ds(pl.multiple_of((at % 16) * unit, 8), unit), :]
-            mod_weight_grad_ref[part * unit : (part + 1) * unit] = kept[:, 0:128]
-            spread_bias[part * unit : (part + 1) * unit] = kept[:, 128:256]
-        mod_bias_grad_ref[...] = spread_bias[...].T[0:1]
+    unit = mod_weight_grad_ref.shape[0] // 6
+    middle = model // 2
+
+    def time_part(m):
         base = place % 16
+        rest = jnp.concatenate([by_vector[m, pl.ds(base, 1)], by_vector[m, pl.ds(base + 16, 1)]], 0)
         both = jnp.zeros((2, 128), jnp.float32)
-        for m in range(6):
-            rest = jnp.concatenate([by_vector[m, pl.ds(base, 1)], by_vector[m, pl.ds(base + 16, 1)]], 0)
-            for _ in range(3):
-                high = rest.astype(jnp.bfloat16)
-                both = both + dot(high, mod_weight_ref[m * model : (m + 1) * model], 1, 0)
-                rest = rest - high.astype(jnp.float32)
-        time_grad_ref[...] = both
-        gains = [jnp.sum(late[:, row, :], 0, keepdims=True) for row in (4, 5)]
-        gains = jnp.concatenate(gains, 1)
-        turned[...] = jnp.concatenate([running[5, 0:6], gains, gains], 0).T
+        for _ in range(3):
+            high = rest.astype(jnp.bfloat16)
+            both = both + dot(high, mod_weight_ref[m * model : (m + 1) * model], 1, 0)
+            rest = rest - high.astype(jnp.float32)
+        return both
+
+    def early_vectors():
+        for m in range(2, 6):
+            by_vector[m, :, 0:middle] = early[:, 2 * m - 4, :]
+            by_vector[m, :, middle:model] = early[:, 2 * m - 3, :]
+        time_grad_ref[...] = sum(time_part(m) for m in range(2, 6))
+        turned[...] = running[5].T
         narrow = turned[pl.ds(pl.multiple_of(dp * unit, 8), unit), :].T
         feed_gain_grad_ref[...] = narrow[0:1]
         down_bias_grad_ref[...] = narrow[1:2]
-        gain_grad_ref[...] = narrow[6:7]
         wide_rows = up_bias_grad_ref.shape[1]
         share_of = model // wide_rows
         wide = turned[pl.ds(pl.multiple_of((dp % share_of) * wide_rows, 8), wide_rows), :].T
@@ -1302,6 +1286,30 @@
         for tile in range(4):
             picked = jnp.where(dp // share_of == tile, wide[2 + tile : 3 + tile], picked)
         up_bias_grad_ref[...] = picked
+
+    def late_vectors():
+        for m in range(2):
+            by_vector[m, :, 0:middle] = late[:, 2 * m, :]
+            by_vector[m, :, middle:model] = late[:, 2 * m + 1, :]
+        ones = jnp.ones((32, 128), jnp.float32)
+        factors = jnp.concatenate([late[:, 6, 0:128], ones], 1)
+        for part in range(6):
+            at = dp * 6 + part
+            spread[...] = lax.dot_general(
+                by_vector[at // 16],
+                factors,
+                (((0,), (0,)), ((), ())),
+                precision=highest,
+                preferred_element_type=jnp.float32,
+            )
+            kept = spread[pl.ds(pl.multiple_of((at % 16) * unit, 8), unit), :]
+            mod_weight_grad_ref[part * unit : (part + 1) * unit] = kept[:, 0:128]
+            spread_bias[part * unit : (part + 1) * unit] = kept[:, 128:256]
+        mod_bias_grad_ref[...] = spread_bias[...].T[0:1]
+        time_grad_ref[...] += time_part(0) + time_part(1)
+        gains = [jnp.sum(late[:, row, :], 0, keepdims=True) for row in (4, 5)]
+        turned[...] = jnp.broadcast_to(jnp.concatenate(gains, 1), (8, model)).T
+        gain_grad_ref[...] = turned[pl.ds(pl.multiple_of(dp * unit, 8), unit), :].T[0:1]
 
     @at_step(6)
     def _():
@@ -1336,6 +1344,7 @@
 
         early_arrive(3)
         running_arrive(4)
+        early_vectors()
         ins[0].last()
         hop_on()
         ins[1].last()
@@ -1343,7 +1352,7 @@
         ins[2].last()
         hop_on()
         hop_on()
-        vectors()
+        late_vectors()
         for group in range(3):
             def store(at, value, group=group):
                 span = 128 * CHUNKS[group]
@@ -1393,7 +1402,7 @@
 def close_kernel(*refs):
     count = len(refs) // 2
     for source, target in zip(refs[:count], refs[count:]):
-        target[...] = source[...]
+        target[...] = source[...].reshape(target.shape)
 
 
 def turn_tables(length):
@@ -1432,7 +1441,11 @@
     shape = jax.ShapeDtypeStruct
 
     packed = [modulation_bias, attention_gain, feed_gain, feed_down_bias, feed_up_bias]
-    packed = jnp.concatenate(packed).astype(f32)[None]
+    total = sum(v.shape[0] for v in packed)
+    starts = np.cumsum([0] + [v.shape[0] for v in packed])
+    packed = sum(
+        lax.pad(v.astype(f32), np.float32(0), [(int(a), int(total - a - v.shape[0]), 0)]) for v, a in zip(packed, starts)
+    )[None]
 
     def packed_at(number):
         return pl.BlockSpec((1, model), lambda h: (0, number), pipeline_mode=pl.Buffered(1))
@@ -1471,9 +1484,9 @@
             pltpu.VMEM((length, 128), f32),
             pltpu.VMEM((length, 128), f32),
             pltpu.VMEM((length, 3 * model), bf16),
-            pltpu.SemaphoreType.DMA((2, half // T_ROWS)),
+            pltpu.SemaphoreType.DMA((2, half // FRONT_ROWS)),
             pltpu.SemaphoreType.DMA((5,)),
-            pltpu.SemaphoreType.DMA((3 * half // T_ROWS,)),
+            pltpu.SemaphoreType.DMA((3 * half // FRONT_ROWS,)),
         ],
         compiler_params=pltpu.CompilerParams(vmem_limit_bytes=62 * MIB, collective_id=2, has_side_effects=True),
         cost_estimate=pl.CostEstimate(flops=2 * length * model * 3 * model, bytes_accessed=16 * MIB, transcendentals=0),
@@ -1750,8 +1763,8 @@
         close_kernel,
         grid=(2,),
         in_specs=[cut(r.shape) for r in results],
-        out_specs=[cut(r.shape) for r in results],
-        out_shape=[shape(r.shape, r.dtype) for r in results],
+        out_specs=[pl.BlockSpec(r.shape[1:], lambda i: (0,)) if r.shape[0] == 1 else cut(r.shape) for r in results],
+        out_shape=[shape(r.shape[1:] if r.shape[0] == 1 else r.shape, r.dtype) for r in results],
         compiler_params=params(62),
         name="close",
     )(*results)
@@ -1760,15 +1773,15 @@
         tokens_grad,
         time_grad,
         modulation_weight_grad,
-        modulation_bias_grad[0],
-        gain_grad[0],
+        modulation_bias_grad,
+        gain_grad,
         in_grad,
         out_grad,
-        feed_gain_grad[0],
+        feed_gain_grad,
         up_grad,
-        feed_up_bias_grad[0],
+        feed_up_bias_grad,
         down_grad,
-        feed_down_bias_grad[0],
+        feed_down_bias_grad,
     )
 
 

time: 217 us -> 213 us (0.982)
  local copies, waits for them, and re-layouts: 3.5 us -> 0.65 us
    unnamed x4 -> x0, local copies, waits for them, and re-layouts: 2.79 us -> none
where the time goes in v3:
time: 213 us; the launch traced here: 212 us
  Pallas kernels  209 us (98%)
    pallas_call x1, Pallas kernels, fast_body(): pl.pallas_call(back_kernel, grid=(pairs + 2,), in_specs=[near(0), near(pa...  81.6 us
    pallas_call x1, Pallas kernels, fast_body(): pl.pallas_call(middle_kernel, grid=(tiles,), in_specs=[own_part, fixed(ha...  76 us
    pallas_call x1, Pallas kernels, fast_body(): pl.pallas_call(front_kernel, grid=(1,), in_specs=[anywhere, fixed(2, 128)...  24.6 us
    pallas_call x1, Pallas kernels, fast_body(): pl.pallas_call(attend_kernel, grid=(pairs,), in_specs=[pl.BlockSpec(memor...  22.8 us

profile of v3, /device:TPU:0, one launch (start us, length us, event | category | flops | bytes accessed | tf_op | source)
XLA Modules:
  0.0 211.6 jit_solution(2102294764284763907)
XLA Ops:
  0.6 0.8 convert_add_fusion
  1.4 0.6 broadcast_in_dim.3.mod_bias_ref.gain_ref.up_bias_ref.down_bias_ref
  2.1 24.6 %front.1 = (bf16[768,1024]{1,0:T(8,128)(2,1)}, bf16[1024,2304]{1,0:T(8,128)(2,1)}, bf16[512,768]{1,0:T(8,128)(2,1)}, f32[6,768]{1,0:T(8,128)}) custom-call(bf16[2,512,768]{2,1,0:T(8,128)(2,1)} %own_hbm.1, bf16[2,128]{1,0:T(2,128)(2,1)} %time_ref.3, bf16[4608,128]{1,0:T(8,128)(2,1)} %mod_weight_hbm.3, ...), custom_call_target="tpu_custom_call" | custom-call | flops 3623878656 | bytes 16777216 | tf_op jit(solution)/shard_map/front/pallas_call | solution.py:1459
  26.7 22.8 %attend.1 = (bf16[1024,768]{1,0:T(8,128)(2,1)}, bf16[12,1024,1024]{2,1,0:T(8,128)(2,1)}, f32[1024,768]{1,0:T(8,128)}, f32[8,512]{1,0:T(8,128)}, f32[8,512]{1,0:T(8,128)}, /*index=5*/bf16[512,768]{1,0:T(8,128)(2,1)}) custom-call(s32[2]{0:T(128)} %prefix_ref.1, bf16[1024,2304]{1,0:T(8,128)(2,1)} %get-tuple-element.61.q_ref.k_ref.v_ref, ...), custom_call_target="tpu_custom_call" | custom-call | flops 12884901888 | bytes 33554432 | tf_op jit(solution)/shard_map/attend/pallas_call | solution.py:1500
  49.5 76.0 %middle.1 = (bf16[2,512,768]{2,1,0:T(8,128)(2,1)}, bf16[512,768]{1,0:T(8,128)(2,1)}, f32[1024,768]{1,0:T(8,128)}, bf16[1024,768]{1,0:T(8,128)(2,1)}, f32[6,768]{...) custom-call(bf16[2,512,768]{2,1,0:T(8,128)(2,1)} %own_hbm.1, ...), custom_call_target="tpu_custom_call" | custom-call | flops 32614907904 | bytes 37748736 | tf_op jit(solution)/shard_map/middle/pallas_call | solution.py:1555
  125.5 81.6 %back.1 = (bf16[2,512,768]{2,1,0:T(8,128)(2,1)}, f32[2,128]{1,0:T(2,128)}, f32[288,128]{1,0:T(8,128)}, f32[1,288]{1,0:T(1,128)}, f32[1,48]{1,0:T(1,128)}, /*inde...) custom-call(bf16[1024,2304]{1,0:T(8,128)(2,1)} %get-tuple-element.61, ...), custom_call_target="tpu_custom_call", output_to_operand_aliasing={{12}: (27, {})} | custom-call | flops 32212254720 | bytes 62914560 | tf_op jit(solution)/shard_map/back/pallas_call | solution.py:1664
  207.1 4.2 %close.1 = (bf16[2,512,768]{2,1,0:T(8,128)(2,1)}, f32[2,128]{1,0:T(2,128)}, f32[288,128]{1,0:T(8,128)}, f32[288]{0:T(512)}, f32[48]{0:T(128)}, /*index=5*/f32[48...) custom-call(bf16[2,512,768]{2,1,0:T(8,128)(2,1)} %get-tuple-element., ...), custom_call_target="tpu_custom_call" | custom-call | tf_op jit(solution)/shard_map/close/pallas_call | solution.py:1762

commit v4 on v3

--- a/solution.py
+++ b/solution.py
@@ -607,7 +607,7 @@
     width = up.shape[1]
     bias_sum = jnp.zeros((1, width), jnp.float32)
     for chunk in range(length // rows):
-        if chunk * rows == half:
+        if chunk == 1:
 
             @pl.when(step > 0)
             def _():
@@ -664,7 +664,7 @@
             grad_attended_ref[at] = dot(grad_one, out_weight_ref[...], 1, 1).astype(jnp.bfloat16)
             for i, term in enumerate((grad_middle * branch, grad, weighted, cot * branch_two)):
                 sums[i] = sums[i] + jnp.sum(term, 0, keepdims=True)
-            if (chunk + 1) * rows == half:
+            if chunk == 0:
                 send_on(last, True)
                 send_down(last - 1)
         rows_ref[0:1] = sums[0]
@@ -1342,6 +1342,7 @@
             if number < 3:
                 start_all(spread_copies(links, late, sems, late_slot, number + 1))
 
+        hop_on()
         early_arrive(3)
         running_arrive(4)
         early_vectors()
@@ -1350,7 +1351,6 @@
         ins[1].last()
         hop_on()
         ins[2].last()
-        hop_on()
         hop_on()
         late_vectors()
         for group in range(3):

time: 213 us -> 211 us (level)
    pallas_call x1, Pallas kernels: 76 us -> 65 us  [fast_body(): pl.pallas_call(middle_kernel, grid=(tiles,), in_specs=[own_part, fixed(ha...]
    pallas_call x1, Pallas kernels: 81.6 us -> 91.2 us  [fast_body(): pl.pallas_call(back_kernel, grid=(pairs + 2,), in_specs=[near(0), near(pa...]
where the time goes in v4:
time: 211 us; the launch traced here: 210 us
  Pallas kernels  208 us (99%)
    pallas_call x1, Pallas kernels, fast_body(): pl.pallas_call(back_kernel, grid=(pairs + 2,), in_specs=[near(0), near(pa...  91.2 us
    pallas_call x1, Pallas kernels, fast_body(): pl.pallas_call(middle_kernel, grid=(tiles,), in_specs=[own_part, fixed(ha...  65 us
    pallas_call x1, Pallas kernels, fast_body(): pl.pallas_call(front_kernel, grid=(1,), in_specs=[anywhere, fixed(2, 128)...  24.6 us
    pallas_call x1, Pallas kernels, fast_body(): pl.pallas_call(attend_kernel, grid=(pairs,), in_specs=[pl.BlockSpec(memor...  22.8 us
    pallas_call x1, Pallas kernels, fast_body(): pl.pallas_call(close_kernel, grid=(2,), in_specs=[cut(r.shape) for r in r...  4.25 us

profile of v4, /device:TPU:0, one launch (start us, length us, event | category | flops | bytes accessed | tf_op | source)
XLA Modules:
  0.0 210.2 jit_solution(7226527001703598699)
XLA Ops:
  0.6 0.8 convert_add_fusion
  1.4 0.6 broadcast_in_dim.3.mod_bias_ref.gain_ref.up_bias_ref.down_bias_ref
  2.1 24.6 %front.1 = (bf16[768,1024]{1,0:T(8,128)(2,1)}, bf16[1024,2304]{1,0:T(8,128)(2,1)}, bf16[512,768]{1,0:T(8,128)(2,1)}, f32[6,768]{1,0:T(8,128)}) custom-call(bf16[2,512,768]{2,1,0:T(8,128)(2,1)} %own_hbm.1, bf16[2,128]{1,0:T(2,128)(2,1)} %time_ref.3, bf16[4608,128]{1,0:T(8,128)(2,1)} %mod_weight_hbm.3, ...), custom_call_target="tpu_custom_call" | custom-call | flops 3623878656 | bytes 16777216 | tf_op jit(solution)/shard_map/front/pallas_call | solution.py:1459
  26.7 22.8 %attend.1 = (bf16[1024,768]{1,0:T(8,128)(2,1)}, bf16[12,1024,1024]{2,1,0:T(8,128)(2,1)}, f32[1024,768]{1,0:T(8,128)}, f32[8,512]{1,0:T(8,128)}, f32[8,512]{1,0:T(8,128)}, /*index=5*/bf16[512,768]{1,0:T(8,128)(2,1)}) custom-call(s32[2]{0:T(128)} %prefix_ref.1, bf16[1024,2304]{1,0:T(8,128)(2,1)} %get-tuple-element.61.q_ref.k_ref.v_ref, ...), custom_call_target="tpu_custom_call" | custom-call | flops 12884901888 | bytes 33554432 | tf_op jit(solution)/shard_map/attend/pallas_call | solution.py:1500
  49.5 65.0 %middle.1 = (bf16[2,512,768]{2,1,0:T(8,128)(2,1)}, bf16[512,768]{1,0:T(8,128)(2,1)}, f32[1024,768]{1,0:T(8,128)}, bf16[1024,768]{1,0:T(8,128)(2,1)}, f32[6,768]{...) custom-call(bf16[2,512,768]{2,1,0:T(8,128)(2,1)} %own_hbm.1, ...), custom_call_target="tpu_custom_call" | custom-call | flops 32614907904 | bytes 37748736 | tf_op jit(solution)/shard_map/middle/pallas_call | solution.py:1555
  114.5 91.2 %back.1 = (bf16[2,512,768]{2,1,0:T(8,128)(2,1)}, f32[2,128]{1,0:T(2,128)}, f32[288,128]{1,0:T(8,128)}, f32[1,288]{1,0:T(1,128)}, f32[1,48]{1,0:T(1,128)}, /*inde...) custom-call(bf16[1024,2304]{1,0:T(8,128)(2,1)} %get-tuple-element.61, ...), custom_call_target="tpu_custom_call", output_to_operand_aliasing={{12}: (27, {})} | custom-call | flops 32212254720 | bytes 62914560 | tf_op jit(solution)/shard_map/back/pallas_call | solution.py:1664
  205.8 4.2 %close.1 = (bf16[2,512,768]{2,1,0:T(8,128)(2,1)}, f32[2,128]{1,0:T(2,128)}, f32[288,128]{1,0:T(8,128)}, f32[288]{0:T(512)}, f32[48]{0:T(128)}, /*index=5*/f32[48...) custom-call(bf16[2,512,768]{2,1,0:T(8,128)(2,1)} %get-tuple-element., ...), custom_call_target="tpu_custom_call" | custom-call | tf_op jit(solution)/shard_map/close/pallas_call | solution.py:1762

commit v5 on v4

--- a/solution.py
+++ b/solution.py
@@ -1656,10 +1656,10 @@
         scratch += piece_scratch(spec)
     def cut(dims):
         if len(dims) == 3:
-            return pl.BlockSpec((1, *dims[1:]), lambda i: (i, 0, 0))
+            return pl.BlockSpec((1, dims[1] // 2, dims[2]), lambda i: (i // 2, i % 2, 0))
         if dims[0] % 16:
             return pl.BlockSpec(dims, lambda i: (0, 0))
-        return pl.BlockSpec((dims[0] // 2, dims[1]), lambda i: (i, 0))
+        return pl.BlockSpec((dims[0] // 2, dims[1]), lambda i: (i // 2, 0))
 
     results = pl.pallas_call(
         back_kernel,
@@ -1761,7 +1761,7 @@
         block_output,
     ) = pl.pallas_call(
         close_kernel,
-        grid=(2,),
+        grid=(4,),
         in_specs=[cut(r.shape) for r in results],
         out_specs=[pl.BlockSpec(r.shape[1:], lambda i: (0,)) if r.shape[0] == 1 else cut(r.shape) for r in results],
         out_shape=[shape(r.shape[1:] if r.shape[0] == 1 else r.shape, r.dtype) for r in results],

time: 211 us -> 213 us (level)
  no operation moved by 1% of the time
where the time goes in v5:
time: 213 us; the launch traced here: 212 us
  Pallas kernels  209 us (98%)
    pallas_call x1, Pallas kernels, fast_body(): pl.pallas_call(back_kernel, grid=(pairs + 2,), in_specs=[near(0), near(pa...  91.2 us
    pallas_call x1, Pallas kernels, fast_body(): pl.pallas_call(middle_kernel, grid=(tiles,), in_specs=[own_part, fixed(ha...  65 us
    pallas_call x1, Pallas kernels, fast_body(): pl.pallas_call(front_kernel, grid=(1,), in_specs=[anywhere, fixed(2, 128)...  24.6 us
    pallas_call x1, Pallas kernels, fast_body(): pl.pallas_call(attend_kernel, grid=(pairs,), in_specs=[pl.BlockSpec(memor...  22.8 us
    pallas_call x1, Pallas kernels, fast_body(): pl.pallas_call(close_kernel, grid=(4,), in_specs=[cut(r.shape) for r in r...  5.55 us

profile of v5, /device:TPU:0, one launch (start us, length us, event | category | flops | bytes accessed | tf_op | source)
XLA Modules:
  0.0 211.5 jit_solution(47277955425071954)
XLA Ops:
  0.6 0.8 convert_add_fusion
  1.4 0.6 broadcast_in_dim.3.mod_bias_ref.gain_ref.up_bias_ref.down_bias_ref
  2.1 24.6 %front.1 = (bf16[768,1024]{1,0:T(8,128)(2,1)}, bf16[1024,2304]{1,0:T(8,128)(2,1)}, bf16[512,768]{1,0:T(8,128)(2,1)}, f32[6,768]{1,0:T(8,128)}) custom-call(bf16[2,512,768]{2,1,0:T(8,128)(2,1)} %own_hbm.1, bf16[2,128]{1,0:T(2,128)(2,1)} %time_ref.3, bf16[4608,128]{1,0:T(8,128)(2,1)} %mod_weight_hbm.3, ...), custom_call_target="tpu_custom_call" | custom-call | flops 3623878656 | bytes 16777216 | tf_op jit(solution)/shard_map/front/pallas_call | solution.py:1459
  26.7 22.8 %attend.1 = (bf16[1024,768]{1,0:T(8,128)(2,1)}, bf16[12,1024,1024]{2,1,0:T(8,128)(2,1)}, f32[1024,768]{1,0:T(8,128)}, f32[8,512]{1,0:T(8,128)}, f32[8,512]{1,0:T(8,128)}, /*index=5*/bf16[512,768]{1,0:T(8,128)(2,1)}) custom-call(s32[2]{0:T(128)} %prefix_ref.1, bf16[1024,2304]{1,0:T(8,128)(2,1)} %get-tuple-element.61.q_ref.k_ref.v_ref, ...), custom_call_target="tpu_custom_call" | custom-call | flops 12884901888 | bytes 33554432 | tf_op jit(solution)/shard_map/attend/pallas_call | solution.py:1500
  49.5 65.0 %middle.1 = (bf16[2,512,768]{2,1,0:T(8,128)(2,1)}, bf16[512,768]{1,0:T(8,128)(2,1)}, f32[1024,768]{1,0:T(8,128)}, bf16[1024,768]{1,0:T(8,128)(2,1)}, f32[6,768]{...) custom-call(bf16[2,512,768]{2,1,0:T(8,128)(2,1)} %own_hbm.1, ...), custom_call_target="tpu_custom_call" | custom-call | flops 32614907904 | bytes 37748736 | tf_op jit(solution)/shard_map/middle/pallas_call | solution.py:1555
  114.5 91.2 %back.1 = (bf16[2,512,768]{2,1,0:T(8,128)(2,1)}, f32[2,128]{1,0:T(2,128)}, f32[288,128]{1,0:T(8,128)}, f32[1,288]{1,0:T(1,128)}, f32[1,48]{1,0:T(1,128)}, /*inde...) custom-call(bf16[1024,2304]{1,0:T(8,128)(2,1)} %get-tuple-element.61, ...), custom_call_target="tpu_custom_call", output_to_operand_aliasing={{12}: (27, {})} | custom-call | flops 32212254720 | bytes 62914560 | tf_op jit(solution)/shard_map/back/pallas_call | solution.py:1664
  205.8 5.6 %close.1 = (bf16[2,512,768]{2,1,0:T(8,128)(2,1)}, f32[2,128]{1,0:T(2,128)}, f32[288,128]{1,0:T(8,128)}, f32[288]{0:T(512)}, f32[48]{0:T(128)}, /*index=5*/f32[48...) custom-call(bf16[2,512,768]{2,1,0:T(8,128)(2,1)} %get-tuple-element., ...), custom_call_target="tpu_custom_call" | custom-call | tf_op jit(solution)/shard_map/close/pallas_call | solution.py:1762
